TPU v7x, 256 devices: a whole 4x4x8 slice. The times are simulated.
256 devices in a mesh: gx: 8 (over z), gy: 32 (over x, y, core).
Axes of the slice: x: 4, y: 4, z: 8, core: 2. Of those that a mesh axis runs over, the one named last changes fastest.
Arguments:
- archive: bfloat16 [1048576, 1024], P(('gx', 'gy')), may hold values from -100 to 100
- sketch: bfloat16 [1024, 256], replicated, may hold values from -0.1875 to 0.1875
Outputs:
- q_rows: bfloat16 [1048576, 256], P(('gx', 'gy'))
- r_factor: float32 [256, 256], replicated
- projection: float32 [1024, 256], P(('gx', 'gy'))
All inputs are finite; a program needn't handle non-finite values.
Results may differ from a plain program's by a relative error of at most 0.0012.
Values sent between devices are 32-bit elements; how exact they have to be, the bound alone decides.
A program may use at most 64 MiB of HBM per device.

v0:
```python
import jax
import jax.numpy as jnp
from jax import lax
from jax.sharding import PartitionSpec as P


def swapped(shard, axis, apart):
    return lax.ppermute(shard, axis, [(i, i ^ 1 << apart) for i in range(lax.axis_size(axis))])


def local(archive, sketch):
    sketched = jnp.dot(archive, sketch, preferred_element_type=jnp.float32)
    local_gram = jnp.dot(sketched.T, sketched, precision=lax.Precision.HIGHEST)
    pixels = archive.shape[0] * lax.axis_size("gx") * lax.axis_size("gy")
    root = jnp.sqrt(jnp.float32(pixels))
    gram = local_gram
    for bit in range(lax.axis_size("gy").bit_length() - 1):
        gram = gram + swapped(gram, "gy", bit)
    for bit in range(lax.axis_size("gx").bit_length() - 1):
        gram = gram + swapped(gram, "gx", bit)
    lower = jnp.linalg.cholesky(gram) / root
    r_factor = lower.T
    q_rows = jax.scipy.linalg.solve_triangular(lower, sketched.T, lower=True).T.astype(jnp.bfloat16)
    shares = archive.shape[1] // (lax.axis_size("gx") * lax.axis_size("gy"))
    term = jnp.einsum("pd,pk->dk", archive, q_rows, preferred_element_type=jnp.float32) / root
    total = lax.psum(term, ("gx", "gy"))
    projection = lax.dynamic_slice_in_dim(total, lax.axis_index(("gx", "gy")) * shares, shares, 0)
    return (q_rows, r_factor, projection)


def solution(mesh):
    return jax.shard_map(
        local,
        mesh=mesh,
        in_specs=(P(("gx", "gy"), None), P()),
        out_specs=(P(("gx", "gy"), None), P(), P(("gx", "gy"), None)),
        check_vma=False,
    )
```

profile of v0, /device:TPU:2, one launch (start us, length us, event | category | flops | bytes accessed | tf_op | source)
XLA Modules:
  0.0 434.3 jit_solution(14658710604440151813)
XLA Ops:
  8.2 5.7 %fusion.14 = f32[4096,256]{1,0:T(8,128)S(1)} fusion(bf16[4096,1024]{1,0:T(8,128)(2,1)} %param.2, bf16[1024,256]{1,0:T(8,128)(2,1)S(1)} %copy-done), kind=kOutput, calls=%fused_computation.37 | convolution fusion | flops 2147483648 | bytes 13107200 | tf_op jit(solution)/shard_map/dot_general | solution.py:12
  14.0 6.7 %fusion.15 = f32[256,256]{0,1:T(8,128)S(1)} fusion(f32[4096,256]{1,0:T(8,128)S(1)} %fusion.14), kind=kOutput, calls=%fused_computation.38 | convolution fusion | flops 3221225472 | bytes 4456448 | tf_op jit(solution)/shard_map/dot_general | solution.py:13
  24.0 6.8 %collective-permute-done.1 = f32[256,256]{0,1:T(8,128)S(1)} collective-permute-done((f32[256,256]{0,1:T(8,128)S(1)}, f32[256,256]{0,1:T(8,128)S(1)}, u32[]{:S(2)}, u32[]{:S(2)}) %collective-permute-start.1) | collective-permute-done | bytes 262176 | tf_op jit(solution)/shard_map/ppermute | solution.py:8
  30.8 3.3 collective-permute-start.2
  34.1 5.8 %collective-permute-done.2 = f32[256,256]{0,1:T(8,128)S(1)} collective-permute-done((f32[256,256]{0,1:T(8,128)S(1)}, f32[256,256]{0,1:T(8,128)S(1)}, u32[]{:S(2)}, u32[]{:S(2)}) %collective-permute-start.2) | collective-permute-done | bytes 262176 | tf_op jit(solution)/shard_map/ppermute | solution.py:8
  40.0 2.4 collective-permute-start.3
  42.3 4.9 %collective-permute-done.3 = f32[256,256]{0,1:T(8,128)S(1)} collective-permute-done((f32[256,256]{0,1:T(8,128)S(1)}, f32[256,256]{0,1:T(8,128)S(1)}, u32[]{:S(2)}, u32[]{:S(2)}) %collective-permute-start.3) | collective-permute-done | bytes 262176 | tf_op jit(solution)/shard_map/ppermute | solution.py:8
  49.1 6.3 %collective-permute-done.4 = f32[256,256]{0,1:T(8,128)S(1)} collective-permute-done((f32[256,256]{0,1:T(8,128)S(1)}, f32[256,256]{0,1:T(8,128)S(1)}, u32[]{:S(2)}, u32[]{:S(2)}) %collective-permute-start.4) | collective-permute-done | bytes 262176 | tf_op jit(solution)/shard_map/ppermute | solution.py:8
  56.9 7.0 %collective-permute-done.5 = f32[256,256]{0,1:T(8,128)S(1)} collective-permute-done((f32[256,256]{0,1:T(8,128)S(1)}, f32[256,256]{0,1:T(8,128)S(1)}, u32[]{:S(2)}, u32[]{:S(2)}) %collective-permute-start.5) | collective-permute-done | bytes 262176 | tf_op jit(solution)/shard_map/ppermute | solution.py:8
  63.9 2.8 collective-permute-start.6
  66.7 7.9 %collective-permute-done.6 = f32[256,256]{0,1:T(8,128)S(1)} collective-permute-done((f32[256,256]{0,1:T(8,128)S(1)}, f32[256,256]{0,1:T(8,128)S(1)}, u32[]{:S(2)}, u32[]{:S(2)}) %collective-permute-start.6) | collective-permute-done | bytes 262176 | tf_op jit(solution)/shard_map/ppermute | solution.py:8
  74.6 11.5 %collective-permute-start.7 = (f32[256,256]{0,1:T(8,128)S(1)}, f32[256,256]{0,1:T(8,128)S(1)}, u32[]{:S(2)}, u32[]{:S(2)}) collective-permute-start(f32[256,256]{0,1:T(8,128)S(1)} %add.61), channel_id=1, source_target_pairs={{0,128},{32,160},{64,192},{96,224},{128,0},{160,32},{192,64},{224,... | collective-permute-start | bytes 786440 | tf_op jit(solution)/shard_map/ppermute | solution.py:8
  86.2 7.2 %collective-permute-done.7 = f32[256,256]{0,1:T(8,128)S(1)} collective-permute-done((f32[256,256]{0,1:T(8,128)S(1)}, f32[256,256]{0,1:T(8,128)S(1)}, u32[]{:S(2)}, u32[]{:S(2)}) %collective-permute-start.7) | collective-permute-done | bytes 262176 | tf_op jit(solution)/shard_map/ppermute | solution.py:8
  93.5 11.7 %cholesky.50 = f32[128,128]{1,0:T(8,128)S(1)} custom-call(f32[128,128]{1,0:T(8,128)S(1)} %cholesky.118), custom_call_target="Cholesky" | custom-call | tf_op jit(solution)/shard_map/jit(cholesky)/cholesky | solution.py:21
  105.3 9.8 %custom-call.15 = f32[1,128,128]{1,2,0:T(8,128)S(1)} custom-call(f32[1,128,128]{2,1,0:T(8,128)S(1)} %get-tuple-element.29), custom_call_target="InvertDiagBlocksLowerTriangular" | custom-call | tf_op jit(solution)/shard_map/jit(cholesky)/cholesky | solution.py:21
  115.6 11.7 %cholesky.105 = f32[128,128]{1,0:T(8,128)S(1)} custom-call(f32[128,128]{1,0:T(8,128)S(1)} %slice_subtract_fusion), custom_call_target="Cholesky" | custom-call | tf_op jit(solution)/shard_map/jit(cholesky)/cholesky | solution.py:21
  129.4 4.2 while.1
  133.6 19.7 %custom-call.16 = f32[2,128,128]{1,2,0:T(8,128)S(1)} custom-call(f32[2,128,128]{2,1,0:T(8,128)S(1)} %get-tuple-element.10), custom_call_target="InvertDiagBlocksLowerTriangular" | custom-call | tf_op jit(solution)/shard_map/jit(_solve_triangular)/triangular_solve | solution.py:23
  153.3 3.7 fusion.13
  157.0 3.5 convolution_subtract_fusion
  160.6 1.9 convolution_convert_fusion
  163.5 6.7 %fusion.2 = f32[1024,256]{0,1:T(8,128)} fusion(bf16[4096,1024]{1,0:T(8,128)(2,1)} %param.2, bf16[128,4096]{1,0:T(8,128)(2,1)S(1)} %convolution_convert_fusion, bf16[128,4096]{1,0:T(8,128)(2,1)S(1)} %get-tuple-element.32), kind=kOutput, calls=%fused_computation.8 | convolution fusion | flops 2151940096 | bytes 11534336 | tf_op jit(solution)/shard_map/pd,pk->dk/dot_general | solution.py:25
  171.9 2.5 copy.8
  175.2 250.2 %all-reduce.3.cloned.1.call-done = f32[1024,256]{0,1:T(8,128)} async-done(((f32[1024,256]{0,1:T(8,128)}), f32[1024,256]{0,1:T(8,128)}) %all-reduce.3.cloned.1.call-update) | async-done | bytes 1048592 | tf_op jit(solution)/shard_map/psum | solution.py:26
  (48 shorter events, 18.5 us)
Async XLA Ops:
  7.2 1.0 copy-start
  7.2 418.2 %all-reduce.3.cloned.1.call-start = ((), (), s32[]{:S(2)}) async-start(), calls=%async_computation | async-start | bytes 2097152 | tf_op jit(solution)/shard_map/psum | solution.py:26
  13.9 6.7 %copy-start.1 = (f32[4096,256]{1,0:T(8,128)}, f32[4096,256]{1,0:T(8,128)S(1)}, u32[]{:S(2)}) copy-start(f32[4096,256]{1,0:T(8,128)S(1)} %fusion.14) | copy-start | bytes 12582916
  20.7 1.6 collective-permute-start
  22.4 8.4 %collective-permute-start.1 = (f32[256,256]{0,1:T(8,128)S(1)}, f32[256,256]{0,1:T(8,128)S(1)}, u32[]{:S(2)}, u32[]{:S(2)}) collective-permute-start(f32[256,256]{0,1:T(8,128)S(1)} %add.55), channel_id=1, source_target_pairs={{0,2},{1,3},{2,0},{3,1},{4,6},{5,7},{6,4},{7,5},{8,10},{9,11},{10,... | collective-permute-start | bytes 786440 | tf_op jit(solution)/shard_map/ppermute | solution.py:8
  30.8 9.1 %collective-permute-start.2 = (f32[256,256]{0,1:T(8,128)S(1)}, f32[256,256]{0,1:T(8,128)S(1)}, u32[]{:S(2)}, u32[]{:S(2)}) collective-permute-start(f32[256,256]{0,1:T(8,128)S(1)} %add.56), channel_id=1, source_target_pairs={{0,4},{1,5},{2,6},{3,7},{4,0},{5,1},{6,2},{7,3},{8,12},{9,13},{10,... | collective-permute-start | bytes 786440 | tf_op jit(solution)/shard_map/ppermute | solution.py:8
  40.0 7.2 %collective-permute-start.3 = (f32[256,256]{0,1:T(8,128)S(1)}, f32[256,256]{0,1:T(8,128)S(1)}, u32[]{:S(2)}, u32[]{:S(2)}) collective-permute-start(f32[256,256]{0,1:T(8,128)S(1)} %add.57), channel_id=1, source_target_pairs={{0,8},{1,9},{2,10},{3,11},{4,12},{5,13},{6,14},{7,15},{8,0},{9,1},... | collective-permute-start | bytes 786440 | tf_op jit(solution)/shard_map/ppermute | solution.py:8
  47.2 8.1 %collective-permute-start.4 = (f32[256,256]{0,1:T(8,128)S(1)}, f32[256,256]{0,1:T(8,128)S(1)}, u32[]{:S(2)}, u32[]{:S(2)}) collective-permute-start(f32[256,256]{0,1:T(8,128)S(1)} %add.58), channel_id=1, source_target_pairs={{0,16},{1,17},{2,18},{3,19},{4,20},{5,21},{6,22},{7,23},{8,24},{9,... | collective-permute-start | bytes 786440 | tf_op jit(solution)/shard_map/ppermute | solution.py:8
  55.4 8.5 %collective-permute-start.5 = (f32[256,256]{0,1:T(8,128)S(1)}, f32[256,256]{0,1:T(8,128)S(1)}, u32[]{:S(2)}, u32[]{:S(2)}) collective-permute-start(f32[256,256]{0,1:T(8,128)S(1)} %add.59), channel_id=1, source_target_pairs={{0,32},{32,0},{64,96},{96,64},{128,160},{160,128},{192,224},{224,1... | collective-permute-start | bytes 786440 | tf_op jit(solution)/shard_map/ppermute | solution.py:8
  63.9 10.7 %collective-permute-start.6 = (f32[256,256]{0,1:T(8,128)S(1)}, f32[256,256]{0,1:T(8,128)S(1)}, u32[]{:S(2)}, u32[]{:S(2)}) collective-permute-start(f32[256,256]{0,1:T(8,128)S(1)} %add.60), channel_id=1, source_target_pairs={{0,64},{32,96},{64,0},{96,32},{128,192},{160,224},{192,128},{224,1... | collective-permute-start | bytes 786440 | tf_op jit(solution)/shard_map/ppermute | solution.py:8
  74.6 18.7 %collective-permute-start.7 = (f32[256,256]{0,1:T(8,128)S(1)}, f32[256,256]{0,1:T(8,128)S(1)}, u32[]{:S(2)}, u32[]{:S(2)}) collective-permute-start(f32[256,256]{0,1:T(8,128)S(1)} %add.61), channel_id=1, source_target_pairs={{0,128},{32,160},{64,192},{96,224},{128,0},{160,32},{192,64},{224,... | collective-permute-start | bytes 786440 | tf_op jit(solution)/shard_map/ppermute | solution.py:8
  153.3 3.7 copy-start.2
  157.0 5.5 %copy-start.4 = (bf16[128,4096]{1,0:T(8,128)(2,1)}, bf16[128,4096]{1,0:T(8,128)(2,1)S(1)}, u32[]{:S(2)}) copy-start(bf16[128,4096]{1,0:T(8,128)(2,1)S(1)} %get-tuple-element.32) | copy-start | bytes 3145732
  162.5 1.0 copy-start.3
Sparse Core Ops, SparseCore 0:
  170.4 255.0 all-reduce.2
where the time goes:
time: 443 us; the launch traced here: 434 us
  waiting for transfers between devices  297 us (67%)
  other arithmetic  55.7 us (13%)
  matrix products  28.8 us (7%)
  starting transfers between devices  25.1 us (6%)
  between operations  15.9 us (4%)
  local copies, waits for them, and re-layouts  11.1 us (3%)
    psum x1, waiting for transfers between devices, local(): total = lax.psum(term, ('gx', 'gy'))  250 us
    ppermute x8, waiting for transfers between devices, swapped(): lax.ppermute(shard, axis, [(i, i ^ 1 << apart) for i in range(lax.axis_si...  47.3 us
    another operation x6, other arithmetic, local(): lower = jnp.linalg.cholesky(gram) / root  33.9 us
    ppermute x8, starting transfers between devices, swapped(): lax.ppermute(shard, axis, [(i, i ^ 1 << apart) for i in range(lax.axis_si...  25.1 us
    another operation x2, other arithmetic, local(): jax.scipy.linalg.solve_triangular(lower, sketched.T, lower=True)  19.7 us
    another operation x3, matrix products, local(): jax.scipy.linalg.solve_triangular(lower, sketched.T, lower=True)  9.15 us
  transfers between devices with their start and end apart: 9, of which 9 were waited for; matrix products, arithmetic and copies ran while one was open for 1% of the time, Pallas kernels for 0%

commit v1 on v0

v1 whole, which is shorter than its diff:
```python
import functools

import jax
import jax.numpy as jnp
from jax import lax
from jax.experimental import pallas as pl
from jax.experimental.pallas import tpu as pltpu
from jax.sharding import PartitionSpec as P

F32, BF16 = jnp.float32, jnp.bfloat16
PARTS = 8
MESH = pl.DeviceIdType.MESH
NT = (((1,), (1,)), ((), ()))


def dot(a, b):
    return jnp.dot(a, b, preferred_element_type=F32)


def dot_nt(a, b):
    return lax.dot_general(a, b, NT, preferred_element_type=F32)


def pieces(value):
    high = value.astype(BF16)
    rest = value - high.astype(F32)
    middle = rest.astype(BF16)
    return high, middle, (rest - middle.astype(F32)).astype(BF16)


def exchange(
    archive_hbm, sketch_hbm, gram_ref, s_hbm, w_ref,
    a, sk, s, hm, acc, wt, g, gcore, gxy, gz, gsum, w, wcore, wxy, wz, wtile,
    a_sem, s_sem, sk_sem, send1, recv1, send2, recv2, send3, recv3, send4, recv4,
    send5, recv5, wsend1, wrecv1, wsend2, wrecv2, wsend3, wrecv3,
):
    z, gy = lax.axis_index("gx"), lax.axis_index("gy")
    core, xy = gy % 2, gy // 2
    rows = a.shape[1]

    def device(zz, xx, cc):
        return (zz, xx * 2 + cc)

    def load(i):
        return pltpu.make_async_copy(
            archive_hbm.at[pl.ds(pl.multiple_of(i * rows, rows), rows), :], a.at[i], a_sem.at[i]
        )

    def save(i):
        return pltpu.make_async_copy(
            s.at[i], s_hbm.at[pl.ds(pl.multiple_of(i * rows, rows), rows), :], s_sem.at[i]
        )

    load_sketch = pltpu.make_async_copy(sketch_hbm, sk, sk_sem)
    load_sketch.start()
    for i in range(PARTS):
        load(i).start()

    barrier = pltpu.get_barrier_semaphore()
    for o in range(1, 16):
        pl.semaphore_signal(barrier, inc=1, device_id=device(z, (xy + o) % 16, core), device_id_type=MESH)
    for o in range(1, 16):
        line = (z * 2 + core + o) % 16
        pl.semaphore_signal(barrier, inc=1, device_id=device(line // 2, xy, line % 2), device_id_type=MESH)

    acc[...] = jnp.zeros_like(acc)
    load_sketch.wait()

    def part(i, carry):
        load(i).wait()
        block = dot(a[i], sk[...])
        s[i] = block
        save(i).start()
        high, middle, low = pieces(block.T)
        hm[i, :256] = high
        hm[i, 256:] = middle
        acc[:768] += dot_nt(jnp.concatenate([high, middle, low], axis=0), high)
        acc[768:] += dot_nt(middle, middle)
        return carry

    lax.fori_loop(0, PARTS, part, 0)
    mixed = acc[256:512] + acc[512:768]
    g[...] = ((acc[:256] + acc[768:]) + (mixed + mixed.T)).reshape(32, 8, 256)

    def remote(src, dst, send, recv, to):
        return pltpu.make_async_remote_copy(
            src_ref=src, dst_ref=dst, send_sem=send, recv_sem=recv, device_id=to, device_id_type=MESH
        )

    other = 1 - core
    sibling = device(z, xy, other)

    def half(ref, which, size):
        return ref.at[pl.ds(pl.multiple_of(which * size, size), size)]

    def cross(b):
        wt[...] = jnp.zeros_like(wt)
        columns = pl.ds(pl.multiple_of(b * 256, 256), 256)

        def step(i, carry):
            both = dot(hm[i], a[i, :, columns])
            wt[...] += both[:256] + both[256:]
            return carry

        lax.fori_loop(0, PARTS, step, 0)
        w[pl.ds(pl.multiple_of(b * 32, 32), 32)] = wt[...].T.reshape(32, 8, 256)

    pl.semaphore_wait(barrier, 30)
    one = remote(half(g, other, 16), gcore, send1, recv1, sibling)
    one.start()
    cross(other * 2)
    one.wait()
    gcore[...] += half(g, core, 16)[...]

    def two(o):
        to = (xy + o) % 16
        return remote(gcore.at[to], gxy.at[o], send2.at[o], recv2.at[o], device(z, to, core))

    for o in range(1, 16):
        two(o).start()
    cross(other * 2 + 1)
    wone = remote(half(w, other, 64), wcore, wsend1, wrecv1, sibling)
    total = gcore[xy]
    for o in range(1, 16):
        two(o).wait_recv()
        total += gxy[o]
    gz[z] = total

    def three(o):
        return remote(gz.at[z], gz.at[z], send3.at[o], recv3.at[z], device((z + o) % 8, xy, core))

    def three_in(o):
        slot = (z + o) % 8
        return remote(gz.at[slot], gz.at[slot], send3.at[o], recv3.at[slot], device(slot, xy, core))

    for o in range(1, 8):
        three(o).start()
    wone.start()
    cross(core * 2)
    for o in range(1, 8):
        three_in(o).wait_recv()
    total = gz[0]
    for o in range(1, 8):
        total += gz[o]
    mine = core * 16 + xy
    gsum[mine] = total

    def four(o):
        return remote(
            gsum.at[mine], gsum.at[mine], send4.at[o], recv4.at[xy], device(z, (xy + o) % 16, core)
        )

    def four_in(o):
        slot = (xy + o) % 16
        there = gsum.at[core * 16 + slot]
        return remote(there, there, send4.at[o], recv4.at[slot], device(z, slot, core))

    for o in range(1, 16):
        four(o).start()
    cross(core * 2 + 1)
    for o in range(1, 16):
        four_in(o).wait_recv()

    five = remote(half(gsum, core, 16), half(gsum, core, 16), send5, recv5, sibling)
    five_in = remote(half(gsum, other, 16), half(gsum, other, 16), send5, recv5, sibling)
    five.start()

    wone.wait()
    wcore[...] += half(w, core, 64)[...]
    for t in range(4):
        for i in range(16):
            wtile[i, t] = wcore[t * 16 + i]

    def wtwo(o):
        to = (xy + o) % 16
        return remote(wtile.at[to], wxy.at[o], wsend2.at[o], wrecv2.at[o], device(z, to, core))

    for o in range(1, 16):
        wtwo(o).start()
    five_in.wait_recv()
    wsum = wtile[xy]
    for o in range(1, 16):
        wtwo(o).wait_recv()
        wsum += wxy[o]
    wcore[:4] = wsum

    def wthree(t, cc):
        to = core * 4 + t
        return remote(
            wcore.at[t], wz.at[z], wsend3.at[t * 2 + cc], wrecv3.at[z], device(to, xy, cc)
        )

    owner = z // 4
    for t in range(4):
        for cc in range(2):
            here = jnp.logical_and(z == core * 4 + t, core == cc)

            @pl.when(jnp.logical_not(here))
            def _():
                wthree(t, cc).start()

            @pl.when(here)
            def _():
                wz[z] = wcore[t]

    for zz in range(8):
        own = jnp.logical_and(z == zz, core == owner)

        @pl.when(jnp.logical_not(own))
        def _():
            remote(
                wcore.at[0], wz.at[zz], wsend3.at[0], wrecv3.at[zz], device(zz, xy, owner)
            ).wait_recv()

    total = wz[0]
    for zz in range(1, 8):
        total += wz[zz]
    w_ref[...] = total
    gram_ref[...] = gsum[...].reshape(256, 256)

    for o in range(1, 16):
        two(o).wait_send()
        four(o).wait_send()
        wtwo(o).wait_send()
    for o in range(1, 8):
        three(o).wait_send()
    five.wait_send()
    for t in range(4):
        for cc in range(2):

            @pl.when(jnp.logical_not(jnp.logical_and(z == core * 4 + t, core == cc)))
            def _():
                wthree(t, cc).wait_send()

    for i in range(PARTS):
        save(i).wait()


def local(archive, sketch):
    pixels, depth = archive.shape
    rank = sketch.shape[1]
    rows = pixels // PARTS
    any_spec = pl.BlockSpec(memory_space=pl.ANY)
    vmem = pl.BlockSpec(memory_space=pltpu.VMEM)
    dma = pltpu.SemaphoreType.DMA
    gram, s, w8 = pl.pallas_call(
        exchange,
        out_shape=(
            jax.ShapeDtypeStruct((rank, rank), F32),
            jax.ShapeDtypeStruct((pixels, rank), F32),
            jax.ShapeDtypeStruct((8, rank), F32),
        ),
        in_specs=[any_spec, any_spec],
        out_specs=(vmem, any_spec, vmem),
        scratch_shapes=[
            pltpu.VMEM((PARTS, rows, depth), BF16),
            pltpu.VMEM((depth, rank), BF16),
            pltpu.VMEM((PARTS, rows, rank), F32),
            pltpu.VMEM((PARTS, 512, rows), BF16),
            pltpu.VMEM((1024, 256), F32),
            pltpu.VMEM((256, 256), F32),
            pltpu.VMEM((32, 8, 256), F32),
            pltpu.VMEM((16, 8, 256), F32),
            pltpu.VMEM((16, 8, 256), F32),
            pltpu.VMEM((8, 8, 256), F32),
            pltpu.VMEM((32, 8, 256), F32),
            pltpu.VMEM((128, 8, 256), F32),
            pltpu.VMEM((64, 8, 256), F32),
            pltpu.VMEM((16, 4, 8, 256), F32),
            pltpu.VMEM((8, 8, 256), F32),
            pltpu.VMEM((16, 4, 8, 256), F32),
            dma((PARTS,)), dma((PARTS,)), dma, dma, dma, dma((16,)), dma((16,)),
            dma((8,)), dma((8,)), dma((16,)), dma((16,)), dma, dma,
            dma, dma, dma((16,)), dma((16,)), dma((8,)), dma((8,)),
        ],
        compiler_params=pltpu.CompilerParams(
            collective_id=0, has_side_effects=True, vmem_limit_bytes=48 * 2**20
        ),
    )(archive, sketch)
    root = jnp.sqrt(F32(pixels * lax.axis_size("gx") * lax.axis_size("gy")))
    lower = jnp.linalg.cholesky(gram) / root
    q_rows = jax.scipy.linalg.solve_triangular(lower, s.T, lower=True).T.astype(BF16)
    both = jax.scipy.linalg.solve_triangular(lower, w8.T, lower=True).T / root
    projection = lax.dynamic_slice_in_dim(both, (lax.axis_index("gy") % 2) * 4, 4, 0)
    return q_rows, lower.T, projection


def solution(mesh):
    return jax.shard_map(
        local,
        mesh=mesh,
        in_specs=(P(("gx", "gy"), None), P()),
        out_specs=(P(("gx", "gy"), None), P(), P(("gx", "gy"), None)),
        check_vma=False,
    )
```

time: 443 us -> 128 us (0.29)
  the two profiles are of different devices: /device:TPU:2 before, /device:TPU:1 now
where the time goes in v1:
time: 128 us
  other arithmetic  54.5 us (43%)
  Pallas kernels  50.8 us (40%)
  local copies, waits for them, and re-layouts  10.4 us (8%)
  matrix products  10.1 us (8%)
  between operations  2.07 us (2%)
    pallas_call x1, Pallas kernels, local(): pl.pallas_call(exchange, out_shape=(jax.ShapeDtypeStruct((rank, rank), F3...  50.8 us
    another operation x6, other arithmetic, local(): lower = jnp.linalg.cholesky(gram) / root  34 us
    another operation x2, other arithmetic, local(): jax.scipy.linalg.solve_triangular(lower, s.T, lower=True).T.astype(BF16)  19.7 us
    another operation x3, matrix products, local(): jax.scipy.linalg.solve_triangular(lower, s.T, lower=True).T.astype(BF16)  9.11 us
    unnamed x8, local copies, waits for them, and re-layouts  6.27 us
    another operation x6, local copies, waits for them, and re-layouts  3.87 us

profile of v1, /device:TPU:1, one launch (start us, length us, event | category | flops | bytes accessed | tf_op | source)
XLA Modules:
  0.0 127.9 jit_solution(1284945058220469732)
XLA Ops:
  0.7 1.0 copy-done.2
  1.8 50.8 %shard_map.49 = (f32[256,256]{1,0:T(8,128)S(1)}, f32[4096,256]{1,0:T(8,128)S(1)}, f32[8,256]{1,0:T(8,128)S(1)}) custom-call(bf16[4096,1024]{1,0:T(8,128)(2,1)} %archive_hbm.1, bf16[1024,256]{1,0:T(8,128)(2,1)S(1)} %copy-done.2), custom_call_target="tpu_custom_call" | custom-call | tf_op jit(solution)/shard_map/pallas_call | solution.py:246
  52.6 1.9 %copy-done = f32[4096,256]{1,0:T(8,128)} copy-done((f32[4096,256]{1,0:T(8,128)}, f32[4096,256]{1,0:T(8,128)S(1)}, u32[]{:S(2)}) %copy-start) | copy-done | bytes 4194328
  54.7 11.7 %cholesky.50 = f32[128,128]{1,0:T(8,128)S(1)} custom-call(f32[128,128]{1,0:T(8,128)S(1)} %cholesky.118), custom_call_target="Cholesky" | custom-call | tf_op jit(solution)/shard_map/jit(cholesky)/cholesky | solution.py:281
  66.5 9.8 %custom-call.18 = f32[1,128,128]{1,2,0:T(8,128)S(1)} custom-call(f32[1,128,128]{2,1,0:T(8,128)S(1)} %get-tuple-element.35), custom_call_target="InvertDiagBlocksLowerTriangular" | custom-call | tf_op jit(solution)/shard_map/jit(cholesky)/cholesky | solution.py:281
  76.3 0.2 constant_dynamic-update-slice_fusion
  76.5 0.3 convolution_subtract_fusion.1
  76.8 11.7 %cholesky.105 = f32[128,128]{1,0:T(8,128)S(1)} custom-call(f32[128,128]{1,0:T(8,128)S(1)} %convolution_subtract_fusion.1), custom_call_target="Cholesky" | custom-call | tf_op jit(solution)/shard_map/jit(cholesky)/cholesky | solution.py:281
  88.5 0.6 compare_reduce_fusion
  90.5 0.8 copy.7
  91.4 3.9 %while.1 = (s32[]{:T(128)}, f32[256,256]{1,0:T(8,128)S(1)}, s32[2,2]{1,0:T(2,128)S(1)}, f32[2,128,128]{2,1,0:T(8,128)S(1)}, s32[]{:T(128)}) while((s32[]{:T(128)}, f32[256,256]{1,0:T(8,128)S(1)}, s32[2,2]{1,0:T(2,128)S(1)}, f32[2,128,128]{2,1,0:T(8,128)S(1)}, s32[]{:T(128)}) %tuple.30), condition=%wide.while_cond, body=%wide.while_body.sunk | while | flops 2 | bytes 131189 | solution.py:282
  91.4 0.6 fusion.25
  92.0 1.3 %bitcast_dynamic-update-slice_fusion.2 = f32[2,128,128]{2,1,0:T(8,128)S(1)} fusion(f32[2,128,128]{2,1,0:T(8,128)S(1)} %get-tuple-element.79, s32[]{:T(128)S(6)} %copy.13, f32[256,256]{1,0:T(8,128)S(1)} %get-tuple-element.82, s32[]{:T(128)} %bitcast.43, s32[]{:T(128)} %bitcast.44), kind=kLoop, calls=%fused_computation.clone.1 | loop fusion | bytes 131084 | tf_op jit(solution)/shard_map/jit(_solve_triangular)/triangular_solve
  93.3 0.6 fusion.25
  93.9 1.3 %bitcast_dynamic-update-slice_fusion.2 = f32[2,128,128]{2,1,0:T(8,128)S(1)} fusion(f32[2,128,128]{2,1,0:T(8,128)S(1)} %get-tuple-element.79, s32[]{:T(128)S(6)} %copy.13, f32[256,256]{1,0:T(8,128)S(1)} %get-tuple-element.82, s32[]{:T(128)} %bitcast.43, s32[]{:T(128)} %bitcast.44), kind=kLoop, calls=%fused_computation.clone.1 | loop fusion | bytes 131084 | tf_op jit(solution)/shard_map/jit(_solve_triangular)/triangular_solve
  95.3 19.7 %custom-call.19 = f32[2,128,128]{1,2,0:T(8,128)S(1)} custom-call(f32[2,128,128]{2,1,0:T(8,128)S(1)} %get-tuple-element.16), custom_call_target="InvertDiagBlocksLowerTriangular" | custom-call | tf_op jit(solution)/shard_map/jit(_solve_triangular)/triangular_solve | solution.py:282
  115.1 0.2 convolution_subtract_fusion.2
  115.3 0.2 fusion.9
  115.5 0.6 fusion.14
  116.1 3.7 %fusion.17 = (bf16[128,4096]{1,0:T(8,128)(2,1)S(1)}, f32[128,4096]{1,0:T(8,128)S(1)}) fusion(f32[256,4096]{0,1:T(8,128)} %bitcast.45, f32[2,128,128]{1,2,0:T(8,128)S(1)} %custom-call.19), kind=kOutput, calls=%fused_computation.41 | convolution fusion | flops 805830656 | bytes 5308416 | tf_op jit(solution)/shard_map/jit(_solve_triangular)/triangular_solve | solution.py:282
  119.8 3.4 %convolution_subtract_fusion = f32[128,4096]{0,1:T(8,128)S(1)} fusion(f32[128,4096]{1,0:T(8,128)S(1)} %get-tuple-element.39, f32[256,4096]{0,1:T(8,128)S(1)} %bitcast.46, f32[256,256]{1,0:T(8,128)S(1)} %get-tuple-element.86), kind=kOutput, calls=%fused_computation.2 | convolution fusion | flops 805830656 | bytes 6356992 | tf_op jit(solution)/shard_map/jit(_solve_triangular)/triangular_solve | solution.py:282
  123.3 2.0 %convolution_convert_fusion = bf16[128,4096]{1,0:T(8,128)(2,1)S(1)} fusion(f32[128,4096]{0,1:T(8,128)S(1)} %convolution_subtract_fusion, f32[2,128,128]{1,2,0:T(8,128)S(1)} %custom-call.19), kind=kOutput, calls=%fused_computation.3 | convolution fusion | flops 805830656 | bytes 3211264 | tf_op jit(solution)/shard_map/jit(_solve_triangular)/triangular_solve | solution.py:282
  125.3 0.2 maximum_bitcast_fusion
  125.4 2.5 %copy.6 = bf16[4096,256]{1,0:T(8,128)(2,1)} copy(bf16[4096,256]{0,1:T(8,128)(2,1)S(1)} %maximum_bitcast_fusion) | data formatting | bytes 4194304
  (17 shorter events, 0.6 us)
Async XLA Ops:
  0.7 1.0 copy-start.2
  52.6 1.9 %copy-start = (f32[4096,256]{1,0:T(8,128)}, f32[4096,256]{1,0:T(8,128)S(1)}, u32[]{:S(2)}) copy-start(f32[4096,256]{1,0:T(8,128)S(1)} %get-tuple-element.7) | copy-start | bytes 12582916
  116.1 3.7 %copy-start.1 = (f32[4096,256]{1,0:T(8,128)S(1)}, f32[4096,256]{1,0:T(8,128)}, u32[]{:S(2)}) copy-start(f32[4096,256]{1,0:T(8,128)} %copy-done) | copy-start | bytes 12582916

commit v2 on v1

--- a/solution.py
+++ b/solution.py
@@ -11,6 +11,7 @@
 PARTS = 8
 MESH = pl.DeviceIdType.MESH
 NT = (((1,), (1,)), ((), ()))
+TN = (((0,), (0,)), ((), ()))
 
 
 def dot(a, b):
@@ -215,7 +216,7 @@
     total = wz[0]
     for zz in range(1, 8):
         total += wz[zz]
-    w_ref[...] = total
+    w_ref[...] = jnp.where(core == 0, total[:4], total[4:])
     gram_ref[...] = gsum[...].reshape(256, 256)
 
     for o in range(1, 16):
@@ -236,6 +237,96 @@
         save(i).wait()
 
 
+def row(tile, j):
+    return jnp.broadcast_to(tile[j : j + 1, :], (8, 128))
+
+
+def column(tile, k):
+    return jnp.broadcast_to(tile[:, k : k + 1], (8, 128))
+
+
+def factor(m):
+    sublane = lax.broadcasted_iota(jnp.int32, (8, 128), 0)
+    for top in range(0, 256, 64):
+        tiles = [0, 1, 2] if top < 128 else [1, 2, 3]
+        at = tiles.index(top // 128)
+
+        def place(g, t):
+            return slice(top + 8 * g, top + 8 * g + 8), slice(128 * t, 128 * t + 128)
+
+        r = [[m[place(g, t)] for t in tiles] for g in range(8)]
+        for s in range(8):
+            lane = (top + 8 * s) % 128
+            c = {(g, k): column(r[g][at], lane + k) for g in range(s, 8) for k in range(8)}
+            scale = jnp.zeros((8, 128), F32)
+            for j in range(8):
+                pivot = row(c[s, j], j)
+                inverse = 1.0 / pivot
+                scale = jnp.where(sublane == j, lax.rsqrt(pivot), scale)
+                for g in range(s, 8):
+                    c[g, j] = c[g, j] * inverse
+                below = jnp.where(sublane > j, c[s, j], 0.0)
+                for k in range(j + 1, 8):
+                    across = row(c[s, k], j)
+                    for g in range(s, 8):
+                        c[g, k] = c[g, k] - c[g, j] * across
+                for t in range(3):
+                    across = row(r[s][t], j)
+                    r[s][t] = r[s][t] - below * across
+                    for g in range(s + 1, 8):
+                        r[g][t] = r[g][t] - c[g, j] * across
+            for t in range(3):
+                r[s][t] = r[s][t] * scale
+        for g in range(8):
+            for i, t in enumerate(tiles):
+                m[place(g, t)] = r[g][i]
+        low = top + 64
+        if low < 256:
+            width = slice(128 * tiles[0], 128 * tiles[0] + 384)
+            hl, ml, ll = pieces(m[top:low, low // 128 * 128 : 256])
+            hp, mp, lp = pieces(m[top:low, width])
+            update = lax.dot_general(
+                jnp.concatenate([hl, hl, ml, ml], axis=0),
+                jnp.concatenate([hp, mp, hp, mp], axis=0),
+                TN, preferred_element_type=F32,
+            )
+            update += lax.dot_general(
+                jnp.concatenate([hl, ll], axis=0), jnp.concatenate([lp, hp], axis=0), TN, preferred_element_type=F32
+            )
+            m[low:, width] -= update[low % 128 :]
+
+
+def finish(root, gram_ref, s_hbm, w_ref, q_hbm, r_ref, p_ref, m, s, q, s_sem, q_sem):
+    rows = s.shape[1]
+
+    def load(i):
+        return pltpu.make_async_copy(s_hbm.at[pl.ds(i * rows, rows), :], s.at[i], s_sem.at[i])
+
+    def save(i):
+        return pltpu.make_async_copy(q.at[i], q_hbm.at[pl.ds(i * rows, rows), :], q_sem.at[i])
+
+    for i in range(PARTS):
+        load(i).start()
+    above = lax.broadcasted_iota(jnp.int32, (256, 256), 1) - lax.broadcasted_iota(jnp.int32, (256, 256), 0)
+    m[:, :256] = gram_ref[...]
+    m[:, 256:] = jnp.where(above == 0, 1.0, 0.0)
+    factor(m)
+    inverse = jnp.where(above <= 0, m[:, 256:], 0.0)
+    high, middle, _ = pieces(inverse * root)
+    both = jnp.concatenate([high, middle, high], axis=1)
+    for i in range(PARTS):
+        load(i).wait()
+        first, second, _ = pieces(s[i])
+        q[i] = dot_nt(jnp.concatenate([first, first, second], axis=1), both).astype(BF16)
+        save(i).start()
+    r_ref[...] = jnp.where(above >= 0, m[:, :256] / root, 0.0)
+    p_ref[...] = lax.dot_general(
+        w_ref[...], inverse, NT, precision=lax.Precision.HIGHEST, preferred_element_type=F32
+    )
+    for i in range(PARTS):
+        save(i).wait()
+
+
 def local(archive, sketch):
     pixels, depth = archive.shape
     rank = sketch.shape[1]
@@ -243,12 +334,12 @@
     any_spec = pl.BlockSpec(memory_space=pl.ANY)
     vmem = pl.BlockSpec(memory_space=pltpu.VMEM)
     dma = pltpu.SemaphoreType.DMA
-    gram, s, w8 = pl.pallas_call(
+    gram, s, w4 = pl.pallas_call(
         exchange,
         out_shape=(
             jax.ShapeDtypeStruct((rank, rank), F32),
             jax.ShapeDtypeStruct((pixels, rank), F32),
-            jax.ShapeDtypeStruct((8, rank), F32),
+            jax.ShapeDtypeStruct((4, rank), F32),
         ),
         in_specs=[any_spec, any_spec],
         out_specs=(vmem, any_spec, vmem),
@@ -277,12 +368,24 @@
             collective_id=0, has_side_effects=True, vmem_limit_bytes=48 * 2**20
         ),
     )(archive, sketch)
-    root = jnp.sqrt(F32(pixels * lax.axis_size("gx") * lax.axis_size("gy")))
-    lower = jnp.linalg.cholesky(gram) / root
-    q_rows = jax.scipy.linalg.solve_triangular(lower, s.T, lower=True).T.astype(BF16)
-    both = jax.scipy.linalg.solve_triangular(lower, w8.T, lower=True).T / root
-    projection = lax.dynamic_slice_in_dim(both, (lax.axis_index("gy") % 2) * 4, 4, 0)
-    return q_rows, lower.T, projection
+    root = float(pixels * lax.axis_size("gx") * lax.axis_size("gy")) ** 0.5
+    return pl.pallas_call(
+        functools.partial(finish, root),
+        out_shape=(
+            jax.ShapeDtypeStruct((pixels, rank), BF16),
+            jax.ShapeDtypeStruct((rank, rank), F32),
+            jax.ShapeDtypeStruct((4, rank), F32),
+        ),
+        in_specs=[vmem, any_spec, vmem],
+        out_specs=(any_spec, vmem, vmem),
+        scratch_shapes=[
+            pltpu.VMEM((rank, 2 * rank), F32),
+            pltpu.VMEM((PARTS, rows, rank), F32),
+            pltpu.VMEM((PARTS, rows, rank), BF16),
+            dma((PARTS,)), dma((PARTS,)),
+        ],
+        compiler_params=pltpu.CompilerParams(vmem_limit_bytes=48 * 2**20),
+    )(gram, s, w4)
 
 
 def solution(mesh):

time: 128 us -> 66.8 us (0.52)
  other arithmetic: 54.5 us -> 0 us
  Pallas kernels: 50.8 us -> 64.8 us
  matrix products: 10.1 us -> 0 us
  local copies, waits for them, and re-layouts: 10.4 us -> 1.03 us
    another operation x8 -> x0, other arithmetic: 53.6 us -> none  [the longest x6 34 us: local(): lower = jnp.linalg.cholesky(gram) / root]
    pallas_call x0 -> x1, Pallas kernels: none -> 14 us  [local(): pl.pallas_call(functools.partial(finish, root), out_shape=(jax.ShapeDtype...]
    another operation x8 -> x0, matrix products: 10.1 us -> none  [the longest x3 9.11 us: local(): jax.scipy.linalg.solve_triangular(lower, s.T, lower=True).T.astype(BF16)]
    unnamed x8 -> x2, local copies, waits for them, and re-layouts: 6.27 us -> 1.03 us
    another operation x9 -> x0, local copies, waits for them, and re-layouts: 3.97 us -> none
where the time goes in v2:
time: 66.8 us; the launch traced here: 66.7 us
  Pallas kernels  64.8 us (97%)
  local copies, waits for them, and re-layouts  1.03 us (2%)
  between operations  0.81 us (1%)
    pallas_call x1, Pallas kernels, local(): pl.pallas_call(exchange, out_shape=(jax.ShapeDtypeStruct((rank, rank), F3...  50.8 us
    pallas_call x1, Pallas kernels, local(): pl.pallas_call(functools.partial(finish, root), out_shape=(jax.ShapeDtype...  14 us

profile of v2, /device:TPU:1, one launch (start us, length us, event | category | flops | bytes accessed | tf_op | source)
XLA Modules:
  0.0 66.7 jit_solution(5537292503433320519)
XLA Ops:
  0.6 0.0 copy-start
  0.6 1.0 %copy-done = bf16[1024,256]{1,0:T(8,128)(2,1)S(1)} copy-done((bf16[1024,256]{1,0:T(8,128)(2,1)S(1)}, bf16[1024,256]{1,0:T(8,128)(2,1)}, u32[]{:S(2)}) %copy-start) | copy-done | bytes 524312
  1.7 50.8 %shard_map.49 = (f32[256,256]{1,0:T(8,128)S(1)}, f32[4096,256]{1,0:T(8,128)S(1)}, f32[4,256]{1,0:T(4,128)S(1)}) custom-call(bf16[4096,1024]{1,0:T(8,128)(2,1)} %archive_hbm.1, bf16[1024,256]{1,0:T(8,128)(2,1)S(1)} %copy-done), custom_call_target="tpu_custom_call" | custom-call | tf_op jit(solution)/shard_map/pallas_call | solution.py:337
  52.5 14.0 %shard_map.50 = (bf16[4096,256]{1,0:T(8,128)(2,1)}, f32[256,256]{1,0:T(8,128)}, f32[4,256]{1,0:T(4,128)}) custom-call(f32[256,256]{1,0:T(8,128)S(1)} %get-tuple-element.6.gram_ref, f32[4096,256]{1,0:T(8,128)S(1)} %get-tuple-element.7.s_hbm, f32[4,256]{1,0:T(4,128)S(1)} %get-tuple-element.8.w_ref), custom_call_target="tpu_custom_call" | custom-call | tf_op jit(solution)/shard_map/pallas_call | solution.py:372
Async XLA Ops:
  0.6 1.0 %copy-start = (bf16[1024,256]{1,0:T(8,128)(2,1)S(1)}, bf16[1024,256]{1,0:T(8,128)(2,1)}, u32[]{:S(2)}) copy-start(bf16[1024,256]{1,0:T(8,128)(2,1)} %sketch_hbm.1) | copy-start | bytes 1572868

commit v3 on v0

v3 whole, which is shorter than its diff:
```python
import functools

import jax
import jax.numpy as jnp
from jax import lax
from jax.experimental import pallas as pl
from jax.experimental.pallas import tpu as pltpu
from jax.sharding import PartitionSpec as P

F32, BF16 = jnp.float32, jnp.bfloat16
PARTS = 2
CHUNKS = 4
MESH = pl.DeviceIdType.MESH
NT = (((1,), (1,)), ((), ()))
TN = (((0,), (0,)), ((), ()))


def dot(a, b):
    return jnp.dot(a, b, preferred_element_type=F32)


def dot_nt(a, b):
    return lax.dot_general(a, b, NT, preferred_element_type=F32)


def pieces(value):
    high = value.astype(BF16)
    rest = value - high.astype(F32)
    middle = rest.astype(BF16)
    return high, middle, (rest - middle.astype(F32)).astype(BF16)


PLANE = sorted(((i // 4, i % 4) for i in range(1, 16)), key=lambda o: -min(o[0], 4 - o[0]) - min(o[1], 4 - o[1]))
LINE = sorted(range(1, 8), key=lambda o: -min(o, 8 - o))


def exchange(
    root, archive_hbm, sketch_hbm, s_hbm, inverse_ref, r_ref, p_ref,
    a, sk, s, hm, g, gcore, gxy, gz, gsum, w, wcore, wtile, wxy, wsum, wz, m,
    a_sem, s_sem, sk_sem, send1, recv1, send2, recv2, send3, recv3, send4, recv4,
    send5, recv5, wsend1, wrecv1, wsend2, wrecv2, wsend3, wrecv3,
):
    z, gy = lax.axis_index("gx"), lax.axis_index("gy")
    core, xy = gy % 2, gy // 2
    x, y = xy // 4, xy % 4
    other = 1 - core
    rows = a.shape[1]

    def device(zz, xx, cc):
        return (zz, xx * 2 + cc)

    def along(o, sign=1):
        return ((x + sign * o[0] + 4) % 4) * 4 + (y + sign * o[1] + 4) % 4

    def remote(src, dst, send, recv, to):
        return pltpu.make_async_remote_copy(
            src_ref=src, dst_ref=dst, send_sem=send, recv_sem=recv, device_id=to, device_id_type=MESH
        )

    def half(ref, which, size):
        return ref.at[pl.ds(pl.multiple_of(which * size, size), size)]

    def load(i):
        return pltpu.make_async_copy(archive_hbm.at[pl.ds(i * rows, rows), :], a.at[i], a_sem.at[i])

    def save(i):
        return pltpu.make_async_copy(s.at[i], s_hbm.at[pl.ds(i * rows, rows), :], s_sem.at[i])

    load_sketch = pltpu.make_async_copy(sketch_hbm, sk, sk_sem)
    load_sketch.start()
    for i in range(PARTS):
        load(i).start()

    barrier = pltpu.get_barrier_semaphore()
    for o in PLANE:
        pl.semaphore_signal(barrier, inc=1, device_id=device(z, along(o), core), device_id_type=MESH)
    for o in LINE:
        for cc in range(2):
            pl.semaphore_signal(barrier, inc=1, device_id=device((z + o) % 8, xy, cc), device_id_type=MESH)
    sibling = device(z, xy, other)
    pl.semaphore_signal(barrier, inc=1, device_id=sibling, device_id_type=MESH)

    load_sketch.wait()
    for i in range(PARTS):
        load(i).wait()
        block = dot(a[i], sk[...])
        s[i] = block
        save(i).start()
        high, middle, _ = pieces(block.T)
        hm[i, :256] = high
        hm[i, 256:] = middle
    both = jnp.concatenate([hm[i] for i in range(PARTS)], axis=1)
    high, middle = both[:256], both[256:]
    first = dot_nt(both, high)
    mixed = first[256:]
    g[...] = ((first[:256] + dot_nt(middle, middle)) + (mixed + mixed.T)).reshape(32, 8, 256)

    def cross(which):
        columns = pl.ds(pl.multiple_of(which * 512, 512), 512)
        both = dot(hm[0], a[0, :, columns])
        for i in range(1, PARTS):
            both += dot(hm[i], a[i, :, columns])
        half(w, which, 64)[...] = (both[:256] + both[256:]).T.reshape(64, 8, 256)

    pl.semaphore_wait(barrier, 30)
    one = remote(half(g, other, 16), gcore, send1, recv1, sibling)
    one.start()
    one.wait()
    gcore[...] += half(g, core, 16)[...]

    def two(i):
        to = along(PLANE[i])
        return remote(gcore.at[to], gxy.at[i], send2.at[i], recv2.at[i], device(z, to, core))

    for i in range(15):
        two(i).start()
    cross(other)
    wone = remote(half(w, other, 64), wcore, wsend1, wrecv1, sibling)
    wone.start()
    cross(core)
    total = gcore[xy]
    for i in reversed(range(15)):
        two(i).wait_recv()
        total += gxy[i]
    gz[z] = total

    def three(i):
        return remote(gz.at[z], gz.at[z], send3.at[i], recv3.at[i], device((z + LINE[i]) % 8, xy, core))

    def three_in(i):
        slot = (z - LINE[i] + 8) % 8
        return remote(gz.at[slot], gz.at[slot], send3.at[i], recv3.at[i], device(slot, xy, core))

    for i in range(7):
        three(i).start()

    wone.wait()
    for t in range(4):
        for i in range(16):
            wtile[i, t] = wcore[t * 16 + i] + w[core * 64 + t * 16 + i]

    def wtwo(i):
        to = along(PLANE[i])
        return remote(wtile.at[to], wxy.at[i], wsend2.at[i], wrecv2.at[i], device(z, to, core))

    for i in range(15):
        wtwo(i).start()

    for i in reversed(range(7)):
        three_in(i).wait_recv()
    total = gz[0]
    for o in range(1, 8):
        total += gz[o]
    mine = core * 16 + xy
    gsum[mine] = total

    def four(i):
        return remote(gsum.at[mine], gsum.at[mine], send4.at[i], recv4.at[i], device(z, along(PLANE[i]), core))

    def four_in(i):
        slot = along(PLANE[i], -1)
        there = gsum.at[core * 16 + slot]
        return remote(there, there, send4.at[i], recv4.at[i], device(z, slot, core))

    for i in range(15):
        four(i).start()
    for i in reversed(range(15)):
        four_in(i).wait_recv()
    five = remote(half(gsum, core, 16), half(gsum, core, 16), send5, recv5, sibling)
    five_in = remote(half(gsum, other, 16), half(gsum, other, 16), send5, recv5, sibling)
    five.start()
    above = lax.broadcasted_iota(jnp.int32, (256, 256), 1) - lax.broadcasted_iota(jnp.int32, (256, 256), 0)
    m[:, 256:] = jnp.where(above == 0, 1.0, 0.0)
    five_in.wait_recv()
    m[:, :256] = gsum[...].reshape(256, 256)

    def wthree(t, cc):
        return remote(
            wsum.at[t], wz.at[z], wsend3.at[t * 2 + cc], wrecv3.at[z], device(core * 4 + t, xy, cc)
        )

    def here(t, cc):
        return jnp.logical_and(z == core * 4 + t, core == cc)

    def along_z():
        total = wtile[xy]
        for i in reversed(range(15)):
            wtwo(i).wait_recv()
            total += wxy[i]
        wsum[...] = total
        for t in range(4):
            for cc in range(2):

                @pl.when(jnp.logical_not(here(t, cc)))
                def _():
                    wthree(t, cc).start()

                @pl.when(here(t, cc))
                def _():
                    wz[z] = wsum[t]

    for top in range(0, 256, 64):
        factor(m, top)
        if top == 64:
            along_z()

    inverse = jnp.where(above <= 0, m[:, 256:], 0.0)
    high, middle, _ = pieces(inverse * root)
    inverse_ref[:, :256] = high
    inverse_ref[:, 256:] = middle
    r_ref[...] = jnp.where(above >= 0, m[:, :256] / root, 0.0)

    owner = z // 4
    for zz in range(8):

        @pl.when(jnp.logical_not(jnp.logical_and(z == zz, core == owner)))
        def _():
            remote(
                wsum.at[0], wz.at[zz], wsend3.at[0], wrecv3.at[zz], device(zz, xy, owner)
            ).wait_recv()

    total = wz[0]
    for zz in range(1, 8):
        total += wz[zz]
    p_ref[...] = lax.dot_general(
        jnp.where(core == 0, total[:4], total[4:]), inverse, NT,
        precision=lax.Precision.HIGHEST, preferred_element_type=F32,
    )

    for i in range(15):
        two(i).wait_send()
        four(i).wait_send()
        wtwo(i).wait_send()
    for i in range(7):
        three(i).wait_send()
    five.wait_send()
    for t in range(4):
        for cc in range(2):

            @pl.when(jnp.logical_not(here(t, cc)))
            def _():
                wthree(t, cc).wait_send()

    for i in range(PARTS):
        save(i).wait()


def row(tile, j):
    return jnp.broadcast_to(tile[j : j + 1, :], (8, 128))


def column(tile, k):
    return jnp.broadcast_to(tile[:, k : k + 1], (8, 128))


def factor(m, top):
    sublane = lax.broadcasted_iota(jnp.int32, (8, 128), 0)
    tiles = [0, 1, 2] if top < 128 else [1, 2, 3]
    at = tiles.index(top // 128)

    def place(g, t):
        return slice(top + 8 * g, top + 8 * g + 8), slice(128 * t, 128 * t + 128)

    r = [[m[place(g, t)] for t in tiles] for g in range(8)]
    for s in range(8):
        lane = (top + 8 * s) % 128
        c = {(g, k): column(r[g][at], lane + k) for g in range(s, 8) for k in range(8)}
        scale = jnp.zeros((8, 128), F32)
        for j in range(8):
            pivot = row(c[s, j], j)
            inverse = 1.0 / pivot
            scale = jnp.where(sublane == j, lax.rsqrt(pivot), scale)
            for g in range(s, 8):
                c[g, j] = c[g, j] * inverse
            below = jnp.where(sublane > j, c[s, j], 0.0)
            for k in range(j + 1, 8):
                across = row(c[s, k], j)
                for g in range(s, 8):
                    c[g, k] = c[g, k] - c[g, j] * across
            for t in range(3):
                across = row(r[s][t], j)
                r[s][t] = r[s][t] - below * across
                for g in range(s + 1, 8):
                    r[g][t] = r[g][t] - c[g, j] * across
        for t in range(3):
            r[s][t] = r[s][t] * scale
    for g in range(8):
        for i, t in enumerate(tiles):
            m[place(g, t)] = r[g][i]
    low = top + 64
    if low < 256:
        width = slice(128 * tiles[0], 128 * tiles[0] + 384)
        hl, ml, ll = pieces(m[top:low, low // 128 * 128 : 256])
        hp, mp, lp = pieces(m[top:low, width])
        update = lax.dot_general(
            jnp.concatenate([hl, hl, ml, ml], axis=0),
            jnp.concatenate([hp, mp, hp, mp], axis=0),
            TN, preferred_element_type=F32,
        )
        update += lax.dot_general(
            jnp.concatenate([hl, ll], axis=0), jnp.concatenate([lp, hp], axis=0), TN, preferred_element_type=F32
        )
        m[low:, width] -= update[low % 128 :]


def finish(inverse_ref, s_hbm, r_hbm, p_hbm, q_hbm, r_out, p_out, s, q, s_sem, q_sem, rp_sem):
    rows = s.shape[1]

    def load(i):
        return pltpu.make_async_copy(s_hbm.at[pl.ds(i * rows, rows), :], s.at[i], s_sem.at[i])

    def save(i):
        return pltpu.make_async_copy(q.at[i], q_hbm.at[pl.ds(i * rows, rows), :], q_sem.at[i])

    for i in range(CHUNKS):
        load(i).start()
    pass_r = pltpu.make_async_copy(r_hbm, r_out, rp_sem.at[0])
    pass_p = pltpu.make_async_copy(p_hbm, p_out, rp_sem.at[1])
    pass_r.start()
    pass_p.start()
    both = inverse_ref[...]
    both = jnp.concatenate([both, both[:, :256]], axis=1)
    for i in range(CHUNKS):
        load(i).wait()
        high, middle, _ = pieces(s[i])
        q[i] = dot_nt(jnp.concatenate([high, high, middle], axis=1), both).astype(BF16)
        save(i).start()
    for i in range(CHUNKS):
        save(i).wait()
    pass_r.wait()
    pass_p.wait()


def local(archive, sketch):
    pixels, depth = archive.shape
    rank = sketch.shape[1]
    rows = pixels // PARTS
    root = float(pixels * lax.axis_size("gx") * lax.axis_size("gy")) ** 0.5
    any_spec = pl.BlockSpec(memory_space=pl.ANY)
    vmem = pl.BlockSpec(memory_space=pltpu.VMEM)
    dma = pltpu.SemaphoreType.DMA
    s, inverse, r_factor, projection = pl.pallas_call(
        functools.partial(exchange, root),
        out_shape=(
            jax.ShapeDtypeStruct((pixels, rank), F32),
            jax.ShapeDtypeStruct((rank, 2 * rank), BF16),
            jax.ShapeDtypeStruct((rank, rank), F32),
            jax.ShapeDtypeStruct((4, rank), F32),
        ),
        in_specs=[any_spec, any_spec],
        out_specs=(any_spec, vmem, vmem, vmem),
        scratch_shapes=[
            pltpu.VMEM((PARTS, rows, depth), BF16),
            pltpu.VMEM((depth, rank), BF16),
            pltpu.VMEM((PARTS, rows, rank), F32),
            pltpu.VMEM((PARTS, 512, rows), BF16),
            pltpu.VMEM((32, 8, 256), F32),
            pltpu.VMEM((16, 8, 256), F32),
            pltpu.VMEM((15, 8, 256), F32),
            pltpu.VMEM((8, 8, 256), F32),
            pltpu.VMEM((32, 8, 256), F32),
            pltpu.VMEM((128, 8, 256), F32),
            pltpu.VMEM((64, 8, 256), F32),
            pltpu.VMEM((16, 4, 8, 256), F32),
            pltpu.VMEM((15, 4, 8, 256), F32),
            pltpu.VMEM((4, 8, 256), F32),
            pltpu.VMEM((8, 8, 256), F32),
            pltpu.VMEM((rank, 2 * rank), F32),
            dma((PARTS,)), dma((PARTS,)), dma, dma, dma, dma((15,)), dma((15,)),
            dma((7,)), dma((7,)), dma((15,)), dma((15,)), dma, dma,
            dma, dma, dma((15,)), dma((15,)), dma((8,)), dma((8,)),
        ],
        compiler_params=pltpu.CompilerParams(
            collective_id=0, has_side_effects=True, vmem_limit_bytes=60 * 2**20
        ),
    )(archive, sketch)
    chunk = pixels // CHUNKS
    return pl.pallas_call(
        finish,
        out_shape=(
            jax.ShapeDtypeStruct((pixels, rank), BF16),
            jax.ShapeDtypeStruct((rank, rank), F32),
            jax.ShapeDtypeStruct((4, rank), F32),
        ),
        in_specs=[vmem, any_spec, any_spec, any_spec],
        out_specs=(any_spec, any_spec, any_spec),
        scratch_shapes=[
            pltpu.VMEM((CHUNKS, chunk, rank), F32),
            pltpu.VMEM((CHUNKS, chunk, rank), BF16),
            dma((CHUNKS,)), dma((CHUNKS,)), dma((2,)),
        ],
        compiler_params=pltpu.CompilerParams(vmem_limit_bytes=60 * 2**20),
    )(inverse, s, r_factor, projection)


def solution(mesh):
    return jax.shard_map(
        local,
        mesh=mesh,
        in_specs=(P(("gx", "gy"), None), P()),
        out_specs=(P(("gx", "gy"), None), P(), P(("gx", "gy"), None)),
        check_vma=False,
    )
```

time: 443 us -> 59.2 us (0.13)
  the two profiles are of different devices: /device:TPU:2 before, /device:TPU:1 now
where the time goes in v3:
time: 59.2 us; the launch traced here: 59.1 us
  Pallas kernels  58.3 us (98%)
  between operations  0.8 us (1%)
    pallas_call x1, Pallas kernels, local(): pl.pallas_call(functools.partial(exchange, root), out_shape=(jax.ShapeDty...  48.1 us
    pallas_call x1, Pallas kernels, local(): pl.pallas_call(finish, out_shape=(jax.ShapeDtypeStruct((pixels, rank), BF...  10.2 us

profile of v3, /device:TPU:1, one launch (start us, length us, event | category | flops | bytes accessed | tf_op | source)
XLA Modules:
  0.0 59.1 jit_solution(16195349182308398908)
XLA Ops:
  0.6 48.1 %shard_map.49 = (f32[4096,256]{1,0:T(8,128)}, bf16[256,512]{1,0:T(8,128)(2,1)}, f32[256,256]{1,0:T(8,128)}, f32[4,256]{1,0:T(4,128)}) custom-call(bf16[4096,1024]{1,0:T(8,128)(2,1)} %archive_hbm.1, bf16[1024,256]{1,0:T(8,128)(2,1)} %sketch_hbm.1), custom_call_target="tpu_custom_call" | custom-call | tf_op jit(solution)/shard_map/pallas_call | solution.py:342
  48.7 10.2 %shard_map.50 = (bf16[4096,256]{1,0:T(8,128)(2,1)}, f32[256,256]{1,0:T(8,128)}, f32[4,256]{1,0:T(4,128)}) custom-call(bf16[256,512]{1,0:T(8,128)(2,1)} %get-tuple-element.7.inverse_ref, f32[4096,256]{1,0:T(8,128)} %get-tuple-element.8.s_hbm, f32[256,256]{1,0:T(8,128)} %get-tuple-element.9.r_hbm, f32[4,256]{1,0:T(4,128)} %get-tuple-element.10.p_hbm), custom_call_target="tpu_custom_call" | custom-call | tf_op jit(solution)/shard_map/pallas_call | solution.py:378

commit v4 on v3

--- a/solution.py
+++ b/solution.py
@@ -35,16 +35,16 @@
 
 
 def exchange(
-    root, archive_hbm, sketch_hbm, s_hbm, inverse_ref, r_ref, p_ref,
-    a, sk, s, hm, g, gcore, gxy, gz, gsum, w, wcore, wtile, wxy, wsum, wz, m,
-    a_sem, s_sem, sk_sem, send1, recv1, send2, recv2, send3, recv3, send4, recv4,
+    root, archive_hbm, sketch_hbm, q_hbm, r_ref, p_ref,
+    a, sk, s, hm, q, g, gcore, gxy, gz, gsum, w, wcore, wtile, wxy, wsum, wz, m,
+    a_sem, q_sem, sk_sem, send1, recv1, send2, recv2, send3, recv3, send4, recv4,
     send5, recv5, wsend1, wrecv1, wsend2, wrecv2, wsend3, wrecv3,
 ):
     z, gy = lax.axis_index("gx"), lax.axis_index("gy")
     core, xy = gy % 2, gy // 2
     x, y = xy // 4, xy % 4
     other = 1 - core
-    rows = a.shape[1]
+    rows, chunk = a.shape[1], q.shape[1]
 
     def device(zz, xx, cc):
         return (zz, xx * 2 + cc)
@@ -64,7 +64,7 @@
         return pltpu.make_async_copy(archive_hbm.at[pl.ds(i * rows, rows), :], a.at[i], a_sem.at[i])
 
     def save(i):
-        return pltpu.make_async_copy(s.at[i], s_hbm.at[pl.ds(i * rows, rows), :], s_sem.at[i])
+        return pltpu.make_async_copy(q.at[i], q_hbm.at[pl.ds(i * chunk, chunk), :], q_sem.at[i])
 
     load_sketch = pltpu.make_async_copy(sketch_hbm, sk, sk_sem)
     load_sketch.start()
@@ -84,8 +84,7 @@
     for i in range(PARTS):
         load(i).wait()
         block = dot(a[i], sk[...])
-        s[i] = block
-        save(i).start()
+        s[pl.ds(i * rows, rows)] = block
         high, middle, _ = pieces(block.T)
         hm[i, :256] = high
         hm[i, 256:] = middle
@@ -171,8 +170,6 @@
     five.start()
     above = lax.broadcasted_iota(jnp.int32, (256, 256), 1) - lax.broadcasted_iota(jnp.int32, (256, 256), 0)
     m[:, 256:] = jnp.where(above == 0, 1.0, 0.0)
-    five_in.wait_recv()
-    m[:, :256] = gsum[...].reshape(256, 256)
 
     def wthree(t, cc):
         return remote(
@@ -199,15 +196,19 @@
                 def _():
                     wz[z] = wsum[t]
 
+    along_z()
+    five_in.wait_recv()
+    m[:, :256] = gsum[...].reshape(256, 256)
     for top in range(0, 256, 64):
         factor(m, top)
-        if top == 64:
-            along_z()
 
     inverse = jnp.where(above <= 0, m[:, 256:], 0.0)
     high, middle, _ = pieces(inverse * root)
-    inverse_ref[:, :256] = high
-    inverse_ref[:, 256:] = middle
+    scaled = jnp.concatenate([high, middle, high], axis=1)
+    for i in range(CHUNKS):
+        high, middle, _ = pieces(s[pl.ds(i * chunk, chunk)])
+        q[i] = dot_nt(jnp.concatenate([high, high, middle], axis=1), scaled).astype(BF16)
+        save(i).start()
     r_ref[...] = jnp.where(above >= 0, m[:, :256] / root, 0.0)
 
     owner = z // 4
@@ -241,7 +242,7 @@
             def _():
                 wthree(t, cc).wait_send()
 
-    for i in range(PARTS):
+    for i in range(CHUNKS):
         save(i).wait()
 
 
@@ -262,16 +263,23 @@
         return slice(top + 8 * g, top + 8 * g + 8), slice(128 * t, 128 * t + 128)
 
     r = [[m[place(g, t)] for t in tiles] for g in range(8)]
+    ahead = [column(r[0][at], top % 128 + k) for k in range(8)]
     for s in range(8):
         lane = (top + 8 * s) % 128
-        c = {(g, k): column(r[g][at], lane + k) for g in range(s, 8) for k in range(8)}
+        c = {(g, k): column(r[g][at], lane + k) for g in range(s + 1, 8) for k in range(8)}
+        for k in range(8):
+            c[s, k] = ahead[k]
+        ahead = [column(r[s + 1][at], lane + 8 + k) for k in range(8)] if s < 7 else []
         scale = jnp.zeros((8, 128), F32)
         for j in range(8):
             pivot = row(c[s, j], j)
             inverse = 1.0 / pivot
             scale = jnp.where(sublane == j, lax.rsqrt(pivot), scale)
+            across = [row(c[s + 1, j], k) for k in range(len(ahead))]
             for g in range(s, 8):
                 c[g, j] = c[g, j] * inverse
+            for k in range(len(ahead)):
+                ahead[k] = ahead[k] - c[s + 1, j] * across[k]
             below = jnp.where(sublane > j, c[s, j], 0.0)
             for k in range(j + 1, 8):
                 across = row(c[s, k], j)
@@ -303,34 +311,6 @@
         m[low:, width] -= update[low % 128 :]
 
 
-def finish(inverse_ref, s_hbm, r_hbm, p_hbm, q_hbm, r_out, p_out, s, q, s_sem, q_sem, rp_sem):
-    rows = s.shape[1]
-
-    def load(i):
-        return pltpu.make_async_copy(s_hbm.at[pl.ds(i * rows, rows), :], s.at[i], s_sem.at[i])
-
-    def save(i):
-        return pltpu.make_async_copy(q.at[i], q_hbm.at[pl.ds(i * rows, rows), :], q_sem.at[i])
-
-    for i in range(CHUNKS):
-        load(i).start()
-    pass_r = pltpu.make_async_copy(r_hbm, r_out, rp_sem.at[0])
-    pass_p = pltpu.make_async_copy(p_hbm, p_out, rp_sem.at[1])
-    pass_r.start()
-    pass_p.start()
-    both = inverse_ref[...]
-    both = jnp.concatenate([both, both[:, :256]], axis=1)
-    for i in range(CHUNKS):
-        load(i).wait()
-        high, middle, _ = pieces(s[i])
-        q[i] = dot_nt(jnp.concatenate([high, high, middle], axis=1), both).astype(BF16)
-        save(i).start()
-    for i in range(CHUNKS):
-        save(i).wait()
-    pass_r.wait()
-    pass_p.wait()
-
-
 def local(archive, sketch):
     pixels, depth = archive.shape
     rank = sketch.shape[1]
@@ -339,21 +319,21 @@
     any_spec = pl.BlockSpec(memory_space=pl.ANY)
     vmem = pl.BlockSpec(memory_space=pltpu.VMEM)
     dma = pltpu.SemaphoreType.DMA
-    s, inverse, r_factor, projection = pl.pallas_call(
+    return pl.pallas_call(
         functools.partial(exchange, root),
         out_shape=(
-            jax.ShapeDtypeStruct((pixels, rank), F32),
-            jax.ShapeDtypeStruct((rank, 2 * rank), BF16),
+            jax.ShapeDtypeStruct((pixels, rank), BF16),
             jax.ShapeDtypeStruct((rank, rank), F32),
             jax.ShapeDtypeStruct((4, rank), F32),
         ),
         in_specs=[any_spec, any_spec],
-        out_specs=(any_spec, vmem, vmem, vmem),
+        out_specs=(any_spec, vmem, vmem),
         scratch_shapes=[
             pltpu.VMEM((PARTS, rows, depth), BF16),
             pltpu.VMEM((depth, rank), BF16),
-            pltpu.VMEM((PARTS, rows, rank), F32),
+            pltpu.VMEM((pixels, rank), F32),
             pltpu.VMEM((PARTS, 512, rows), BF16),
+            pltpu.VMEM((CHUNKS, pixels // CHUNKS, rank), BF16),
             pltpu.VMEM((32, 8, 256), F32),
             pltpu.VMEM((16, 8, 256), F32),
             pltpu.VMEM((15, 8, 256), F32),
@@ -366,7 +346,7 @@
             pltpu.VMEM((4, 8, 256), F32),
             pltpu.VMEM((8, 8, 256), F32),
             pltpu.VMEM((rank, 2 * rank), F32),
-            dma((PARTS,)), dma((PARTS,)), dma, dma, dma, dma((15,)), dma((15,)),
+            dma((PARTS,)), dma((CHUNKS,)), dma, dma, dma, dma((15,)), dma((15,)),
             dma((7,)), dma((7,)), dma((15,)), dma((15,)), dma, dma,
             dma, dma, dma((15,)), dma((15,)), dma((8,)), dma((8,)),
         ],
@@ -374,23 +354,6 @@
             collective_id=0, has_side_effects=True, vmem_limit_bytes=60 * 2**20
         ),
     )(archive, sketch)
-    chunk = pixels // CHUNKS
-    return pl.pallas_call(
-        finish,
-        out_shape=(
-            jax.ShapeDtypeStruct((pixels, rank), BF16),
-            jax.ShapeDtypeStruct((rank, rank), F32),
-            jax.ShapeDtypeStruct((4, rank), F32),
-        ),
-        in_specs=[vmem, any_spec, any_spec, any_spec],
-        out_specs=(any_spec, any_spec, any_spec),
-        scratch_shapes=[
-            pltpu.VMEM((CHUNKS, chunk, rank), F32),
-            pltpu.VMEM((CHUNKS, chunk, rank), BF16),
-            dma((CHUNKS,)), dma((CHUNKS,)), dma((2,)),
-        ],
-        compiler_params=pltpu.CompilerParams(vmem_limit_bytes=60 * 2**20),
-    )(inverse, s, r_factor, projection)
 
 
 def solution(mesh):

time: 59.2 us -> 55 us (0.929)
  Pallas kernels: 58.3 us -> 49.8 us
  local copies, waits for them, and re-layouts: 0 us -> 4.39 us
    pallas_call x1 -> x0, Pallas kernels: 10.2 us -> none  [local(): pl.pallas_call(finish, out_shape=(jax.ShapeDtypeStruct((pixels, rank), BF...]
    unnamed x0 -> x7, local copies, waits for them, and re-layouts: none -> 4.39 us
    pallas_call x1, Pallas kernels: 48.1 us -> 49.8 us  [local(): pl.pallas_call(functools.partial(exchange, root), out_shape=(jax.ShapeDty...]
where the time goes in v4:
time: 55 us; the launch traced here: 54.9 us
  Pallas kernels  49.8 us (91%)
  local copies, waits for them, and re-layouts  4.39 us (8%)
  between operations  0.66 us (1%)
    pallas_call x1, Pallas kernels, local(): pl.pallas_call(functools.partial(exchange, root), out_shape=(jax.ShapeDty...  49.8 us
    unnamed x7, local copies, waits for them, and re-layouts  4.39 us

profile of v4, /device:TPU:1, one launch (start us, length us, event | category | flops | bytes accessed | tf_op | source)
XLA Modules:
  0.0 54.9 jit_solution(7242549270471515936)
XLA Ops:
  0.6 49.8 %shard_map.49 = (bf16[4096,256]{1,0:T(8,128)(2,1)}, f32[256,256]{1,0:T(8,128)}, f32[4,256]{1,0:T(4,128)}) custom-call(bf16[4096,1024]{1,0:T(8,128)(2,1)} %archive_hbm.1, bf16[1024,256]{1,0:T(8,128)(2,1)} %sketch_hbm.1), custom_call_target="tpu_custom_call" | custom-call | tf_op jit(solution)/shard_map/pallas_call | solution.py:322
  50.4 0.0 copy-start
  50.5 0.0 copy-start.1
  50.5 3.1 %copy.8 = bf16[4096,256]{1,0:T(8,128)(2,1)} copy(bf16[4096,256]{1,0:T(8,128)(2,1)} %get-tuple-element.6) | data formatting | bytes 4194304
  53.5 0.0 copy-done
  53.6 0.7 %copy.9 = f32[256,256]{1,0:T(8,128)} copy(f32[256,256]{1,0:T(8,128)S(1)} %copy-done) | data formatting | bytes 524288
  54.3 0.0 copy-done.1
  54.3 0.6 %copy.10 = f32[4,256]{1,0:T(4,128)} copy(f32[4,256]{1,0:T(4,128)S(1)} %copy-done.1) | data formatting | bytes 8192
Async XLA Ops:
  50.4 3.1 %copy-start = (f32[256,256]{1,0:T(8,128)S(1)}, f32[256,256]{1,0:T(8,128)}, u32[]{:S(2)}) copy-start(f32[256,256]{1,0:T(8,128)} %get-tuple-element.7) | copy-start | bytes 786436
  50.5 3.8 %copy-start.1 = (f32[4,256]{1,0:T(4,128)S(1)}, f32[4,256]{1,0:T(4,128)}, u32[]{:S(2)}) copy-start(f32[4,256]{1,0:T(4,128)} %get-tuple-element.8) | copy-start | bytes 12292

commit v5 on v4

--- a/solution.py
+++ b/solution.py
@@ -35,16 +35,16 @@
 
 
 def exchange(
-    root, archive_hbm, sketch_hbm, q_hbm, r_ref, p_ref,
-    a, sk, s, hm, q, g, gcore, gxy, gz, gsum, w, wcore, wtile, wxy, wsum, wz, m,
-    a_sem, q_sem, sk_sem, send1, recv1, send2, recv2, send3, recv3, send4, recv4,
+    root, archive_hbm, sketch_hbm, q_ref, r_ref, p_ref,
+    a, sk, s, hm, g, gcore, gxy, gz, gsum, w, wcore, wtile, wxy, wsum, wz, m,
+    a_sem, sk_sem, send1, recv1, send2, recv2, send3, recv3, send4, recv4,
     send5, recv5, wsend1, wrecv1, wsend2, wrecv2, wsend3, wrecv3,
 ):
     z, gy = lax.axis_index("gx"), lax.axis_index("gy")
     core, xy = gy % 2, gy // 2
     x, y = xy // 4, xy % 4
     other = 1 - core
-    rows, chunk = a.shape[1], q.shape[1]
+    rows, chunk = a.shape[1], s.shape[0] // CHUNKS
 
     def device(zz, xx, cc):
         return (zz, xx * 2 + cc)
@@ -62,9 +62,6 @@
 
     def load(i):
         return pltpu.make_async_copy(archive_hbm.at[pl.ds(i * rows, rows), :], a.at[i], a_sem.at[i])
-
-    def save(i):
-        return pltpu.make_async_copy(q.at[i], q_hbm.at[pl.ds(i * chunk, chunk), :], q_sem.at[i])
 
     load_sketch = pltpu.make_async_copy(sketch_hbm, sk, sk_sem)
     load_sketch.start()
@@ -84,10 +81,10 @@
     for i in range(PARTS):
         load(i).wait()
         block = dot(a[i], sk[...])
+        high, middle, _ = pieces(block)
+        block = jnp.concatenate([high, middle], axis=1)
         s[pl.ds(i * rows, rows)] = block
-        high, middle, _ = pieces(block.T)
-        hm[i, :256] = high
-        hm[i, 256:] = middle
+        hm[i] = block.T
     both = jnp.concatenate([hm[i] for i in range(PARTS)], axis=1)
     high, middle = both[:256], both[256:]
     first = dot_nt(both, high)
@@ -204,11 +201,12 @@
 
     inverse = jnp.where(above <= 0, m[:, 256:], 0.0)
     high, middle, _ = pieces(inverse * root)
-    scaled = jnp.concatenate([high, middle, high], axis=1)
+    scaled = jnp.concatenate([high, high, middle], axis=1)
     for i in range(CHUNKS):
-        high, middle, _ = pieces(s[pl.ds(i * chunk, chunk)])
-        q[i] = dot_nt(jnp.concatenate([high, high, middle], axis=1), scaled).astype(BF16)
-        save(i).start()
+        block = s[pl.ds(i * chunk, chunk)]
+        q_ref[pl.ds(i * chunk, chunk)] = dot_nt(
+            jnp.concatenate([block, block[:, :256]], axis=1), scaled
+        ).astype(BF16)
     r_ref[...] = jnp.where(above >= 0, m[:, :256] / root, 0.0)
 
     owner = z // 4
@@ -241,9 +239,6 @@
             @pl.when(jnp.logical_not(here(t, cc)))
             def _():
                 wthree(t, cc).wait_send()
-
-    for i in range(CHUNKS):
-        save(i).wait()
 
 
 def row(tile, j):
@@ -311,6 +306,17 @@
         m[low:, width] -= update[low % 128 :]
 
 
+def deliver(q, r, p, q_hbm, r_hbm, p_hbm, sem):
+    copies = [
+        pltpu.make_async_copy(src, dst, sem.at[i])
+        for i, (src, dst) in enumerate([(q, q_hbm), (r, r_hbm), (p, p_hbm)])
+    ]
+    for copy in copies:
+        copy.start()
+    for copy in copies:
+        copy.wait()
+
+
 def local(archive, sketch):
     pixels, depth = archive.shape
     rank = sketch.shape[1]
@@ -319,21 +325,20 @@
     any_spec = pl.BlockSpec(memory_space=pl.ANY)
     vmem = pl.BlockSpec(memory_space=pltpu.VMEM)
     dma = pltpu.SemaphoreType.DMA
-    return pl.pallas_call(
+    results = pl.pallas_call(
         functools.partial(exchange, root),
         out_shape=(
-            jax.ShapeDtypeStruct((pixels, rank), BF16),
-            jax.ShapeDtypeStruct((rank, rank), F32),
-            jax.ShapeDtypeStruct((4, rank), F32),
+            pltpu.VMEM((pixels, rank), BF16),
+            pltpu.VMEM((rank, rank), F32),
+            pltpu.VMEM((4, rank), F32),
         ),
         in_specs=[any_spec, any_spec],
-        out_specs=(any_spec, vmem, vmem),
+        out_specs=(vmem, vmem, vmem),
         scratch_shapes=[
             pltpu.VMEM((PARTS, rows, depth), BF16),
             pltpu.VMEM((depth, rank), BF16),
-            pltpu.VMEM((pixels, rank), F32),
+            pltpu.VMEM((pixels, 2 * rank), BF16),
             pltpu.VMEM((PARTS, 512, rows), BF16),
-            pltpu.VMEM((CHUNKS, pixels // CHUNKS, rank), BF16),
             pltpu.VMEM((32, 8, 256), F32),
             pltpu.VMEM((16, 8, 256), F32),
             pltpu.VMEM((15, 8, 256), F32),
@@ -346,14 +351,22 @@
             pltpu.VMEM((4, 8, 256), F32),
             pltpu.VMEM((8, 8, 256), F32),
             pltpu.VMEM((rank, 2 * rank), F32),
-            dma((PARTS,)), dma((CHUNKS,)), dma, dma, dma, dma((15,)), dma((15,)),
+            dma((PARTS,)), dma, dma, dma, dma((15,)), dma((15,)),
             dma((7,)), dma((7,)), dma((15,)), dma((15,)), dma, dma,
             dma, dma, dma((15,)), dma((15,)), dma((8,)), dma((8,)),
         ],
         compiler_params=pltpu.CompilerParams(
-            collective_id=0, has_side_effects=True, vmem_limit_bytes=60 * 2**20
+            collective_id=0, has_side_effects=True, vmem_limit_bytes=52 * 2**20
         ),
     )(archive, sketch)
+    return pl.pallas_call(
+        deliver,
+        out_shape=tuple(jax.ShapeDtypeStruct(r.shape, r.dtype) for r in results),
+        in_specs=[vmem] * 3,
+        out_specs=(any_spec,) * 3,
+        scratch_shapes=[dma((3,))],
+        compiler_params=pltpu.CompilerParams(vmem_limit_bytes=4 * 2**20),
+    )(*results)
 
 
 def solution(mesh):

time: 55 us -> 51.1 us (0.929)
  local copies, waits for them, and re-layouts: 4.39 us -> 0 us
    unnamed x7 -> x0, local copies, waits for them, and re-layouts: 4.39 us -> none
    pallas_call x1 -> x2, Pallas kernels: 49.8 us -> 50.2 us  [the longest x1 48.8 us: local(): pl.pallas_call(functools.partial(exchange, root), out_shape=(pltpu.VMEM((...]
where the time goes in v5:
time: 51.1 us; the launch traced here: 51 us
  Pallas kernels  50.2 us (98%)
  between operations  0.8 us (2%)
    pallas_call x1, Pallas kernels, local(): pl.pallas_call(functools.partial(exchange, root), out_shape=(pltpu.VMEM((...  48.8 us
    pallas_call x1, Pallas kernels, local(): pl.pallas_call(deliver, out_shape=tuple((jax.ShapeDtypeStruct(r.shape, r....  1.42 us

profile of v5, /device:TPU:1, one launch (start us, length us, event | category | flops | bytes accessed | tf_op | source)
XLA Modules:
  0.0 51.0 jit_solution(2646650430666236934)
XLA Ops:
  0.6 48.8 %shard_map.49 = (bf16[4096,256]{1,0:T(8,128)(2,1)S(1)}, f32[256,256]{1,0:T(8,128)S(1)}, f32[4,256]{1,0:T(4,128)S(1)}) custom-call(bf16[4096,1024]{1,0:T(8,128)(2,1)} %archive_hbm.1, bf16[1024,256]{1,0:T(8,128)(2,1)} %sketch_hbm.1), custom_call_target="tpu_custom_call" | custom-call | tf_op jit(solution)/shard_map/pallas_call | solution.py:328
  49.4 1.4 %shard_map.50 = (bf16[4096,256]{1,0:T(8,128)(2,1)}, f32[256,256]{1,0:T(8,128)}, f32[4,256]{1,0:T(4,128)}) custom-call(bf16[4096,256]{1,0:T(8,128)(2,1)S(1)} %get-tuple-element.6.q, f32[256,256]{1,0:T(8,128)S(1)} %get-tuple-element.7.r, f32[4,256]{1,0:T(4,128)S(1)} %get-tuple-element.8.p), custom_call_target="tpu_custom_call" | custom-call | tf_op jit(solution)/shard_map/pallas_call | solution.py:362

commit v6 on v5

--- a/solution.py
+++ b/solution.py
@@ -8,7 +8,7 @@
 from jax.sharding import PartitionSpec as P
 
 F32, BF16 = jnp.float32, jnp.bfloat16
-PARTS = 2
+SPLIT = (0, 3072, 4096)
 CHUNKS = 4
 MESH = pl.DeviceIdType.MESH
 NT = (((1,), (1,)), ((), ()))
@@ -44,7 +44,8 @@
     core, xy = gy % 2, gy // 2
     x, y = xy // 4, xy % 4
     other = 1 - core
-    rows, chunk = a.shape[1], s.shape[0] // CHUNKS
+    chunk = s.shape[0] // CHUNKS
+    parts = [slice(i, j) for i, j in zip(SPLIT, SPLIT[1:])]
 
     def device(zz, xx, cc):
         return (zz, xx * 2 + cc)
@@ -61,11 +62,11 @@
         return ref.at[pl.ds(pl.multiple_of(which * size, size), size)]
 
     def load(i):
-        return pltpu.make_async_copy(archive_hbm.at[pl.ds(i * rows, rows), :], a.at[i], a_sem.at[i])
+        return pltpu.make_async_copy(archive_hbm.at[parts[i]], a.at[parts[i]], a_sem.at[i])
 
     load_sketch = pltpu.make_async_copy(sketch_hbm, sk, sk_sem)
     load_sketch.start()
-    for i in range(PARTS):
+    for i in range(len(parts)):
         load(i).start()
 
     barrier = pltpu.get_barrier_semaphore()
@@ -78,29 +79,30 @@
     pl.semaphore_signal(barrier, inc=1, device_id=sibling, device_id_type=MESH)
 
     load_sketch.wait()
-    for i in range(PARTS):
+    for i, part in enumerate(parts):
         load(i).wait()
-        block = dot(a[i], sk[...])
-        high, middle, _ = pieces(block)
+        high, middle, _ = pieces(dot(a[part], sk[...]))
         block = jnp.concatenate([high, middle], axis=1)
-        s[pl.ds(i * rows, rows)] = block
-        hm[i] = block.T
-    both = jnp.concatenate([hm[i] for i in range(PARTS)], axis=1)
-    high, middle = both[:256], both[256:]
-    first = dot_nt(both, high)
-    mixed = first[256:]
-    g[...] = ((first[:256] + dot_nt(middle, middle)) + (mixed + mixed.T)).reshape(32, 8, 256)
+        s[part] = block
+        hm[:, part] = block.T
+
+    def gram(which):
+        first = pl.multiple_of(which * 128, 128)
+        mine = jnp.concatenate([hm[pl.ds(first, 128)], hm[pl.ds(first + 256, 128)]], axis=0)
+        four = dot_nt(mine, hm[...])
+        four = four[:, :256] + four[:, 256:]
+        half(g, which, 16)[...] = (four[:128] + four[128:]).reshape(16, 8, 256)
 
     def cross(which):
         columns = pl.ds(pl.multiple_of(which * 512, 512), 512)
-        both = dot(hm[0], a[0, :, columns])
-        for i in range(1, PARTS):
-            both += dot(hm[i], a[i, :, columns])
+        both = dot(hm[...], a[:, columns])
         half(w, which, 64)[...] = (both[:256] + both[256:]).T.reshape(64, 8, 256)
 
+    gram(other)
     pl.semaphore_wait(barrier, 30)
     one = remote(half(g, other, 16), gcore, send1, recv1, sibling)
     one.start()
+    gram(core)
     one.wait()
     gcore[...] += half(g, core, 16)[...]
 
@@ -320,7 +322,6 @@
 def local(archive, sketch):
     pixels, depth = archive.shape
     rank = sketch.shape[1]
-    rows = pixels // PARTS
     root = float(pixels * lax.axis_size("gx") * lax.axis_size("gy")) ** 0.5
     any_spec = pl.BlockSpec(memory_space=pl.ANY)
     vmem = pl.BlockSpec(memory_space=pltpu.VMEM)
@@ -335,10 +336,10 @@
         in_specs=[any_spec, any_spec],
         out_specs=(vmem, vmem, vmem),
         scratch_shapes=[
-            pltpu.VMEM((PARTS, rows, depth), BF16),
+            pltpu.VMEM((pixels, depth), BF16),
             pltpu.VMEM((depth, rank), BF16),
             pltpu.VMEM((pixels, 2 * rank), BF16),
-            pltpu.VMEM((PARTS, 512, rows), BF16),
+            pltpu.VMEM((2 * rank, pixels), BF16),
             pltpu.VMEM((32, 8, 256), F32),
             pltpu.VMEM((16, 8, 256), F32),
             pltpu.VMEM((15, 8, 256), F32),
@@ -351,7 +352,7 @@
             pltpu.VMEM((4, 8, 256), F32),
             pltpu.VMEM((8, 8, 256), F32),
             pltpu.VMEM((rank, 2 * rank), F32),
-            dma((PARTS,)), dma, dma, dma, dma((15,)), dma((15,)),
+            dma((len(SPLIT) - 1,)), dma, dma, dma, dma((15,)), dma((15,)),
             dma((7,)), dma((7,)), dma((15,)), dma((15,)), dma, dma,
             dma, dma, dma((15,)), dma((15,)), dma((8,)), dma((8,)),
         ],

time: 51.1 us -> 48.3 us (0.945)
  Pallas kernels: 50.2 us -> 47.4 us
    pallas_call x1, Pallas kernels: 48.8 us -> 46 us  [local(): pl.pallas_call(functools.partial(exchange, root), out_shape=(pltpu.VMEM((...]
where the time goes in v6:
time: 48.3 us; the launch traced here: 48.2 us
  Pallas kernels  47.4 us (98%)
  between operations  0.8 us (2%)
    pallas_call x1, Pallas kernels, local(): pl.pallas_call(functools.partial(exchange, root), out_shape=(pltpu.VMEM((...  46 us
    pallas_call x1, Pallas kernels, local(): pl.pallas_call(deliver, out_shape=tuple((jax.ShapeDtypeStruct(r.shape, r....  1.42 us

profile of v6, /device:TPU:1, one launch (start us, length us, event | category | flops | bytes accessed | tf_op | source)
XLA Modules:
  0.0 48.2 jit_solution(14095529536091454587)
XLA Ops:
  0.6 46.0 %shard_map.49 = (bf16[4096,256]{1,0:T(8,128)(2,1)S(1)}, f32[256,256]{1,0:T(8,128)S(1)}, f32[4,256]{1,0:T(4,128)S(1)}) custom-call(bf16[4096,1024]{1,0:T(8,128)(2,1)} %archive_hbm.1, bf16[1024,256]{1,0:T(8,128)(2,1)} %sketch_hbm.1), custom_call_target="tpu_custom_call" | custom-call | tf_op jit(solution)/shard_map/pallas_call | solution.py:329
  46.6 1.4 %shard_map.50 = (bf16[4096,256]{1,0:T(8,128)(2,1)}, f32[256,256]{1,0:T(8,128)}, f32[4,256]{1,0:T(4,128)}) custom-call(bf16[4096,256]{1,0:T(8,128)(2,1)S(1)} %get-tuple-element.6.q, f32[256,256]{1,0:T(8,128)S(1)} %get-tuple-element.7.r, f32[4,256]{1,0:T(4,128)S(1)} %get-tuple-element.8.p), custom_call_target="tpu_custom_call" | custom-call | tf_op jit(solution)/shard_map/pallas_call | solution.py:363

commit v7 on v6

--- a/solution.py
+++ b/solution.py
@@ -8,8 +8,9 @@
 from jax.sharding import PartitionSpec as P
 
 F32, BF16 = jnp.float32, jnp.bfloat16
-SPLIT = (0, 3072, 4096)
+SPLIT = (0, 2048, 3072, 4096)
 CHUNKS = 4
+EARLY = 1
 MESH = pl.DeviceIdType.MESH
 NT = (((1,), (1,)), ((), ()))
 TN = (((0,), (0,)), ((), ()))
@@ -34,9 +35,13 @@
 LINE = sorted(range(1, 8), key=lambda o: -min(o, 8 - o))
 
 
+def basis(block, scaled):
+    return dot_nt(jnp.concatenate([block, block[:, :256]], axis=1), scaled).astype(BF16)
+
+
 def exchange(
-    root, archive_hbm, sketch_hbm, q_ref, r_ref, p_ref,
-    a, sk, s, hm, g, gcore, gxy, gz, gsum, w, wcore, wtile, wxy, wsum, wz, m,
+    root, archive_hbm, sketch_hbm, q_ref, s, scaled_ref, r_ref, p_ref,
+    a, sk, hm, g, gcore, gxy, gz, gsum, w, wcore, wtile, wxy, wsum, wz, m,
     a_sem, sk_sem, send1, recv1, send2, recv2, send3, recv3, send4, recv4,
     send5, recv5, wsend1, wrecv1, wsend2, wrecv2, wsend3, wrecv3,
 ):
@@ -203,12 +208,9 @@
 
     inverse = jnp.where(above <= 0, m[:, 256:], 0.0)
     high, middle, _ = pieces(inverse * root)
-    scaled = jnp.concatenate([high, high, middle], axis=1)
-    for i in range(CHUNKS):
-        block = s[pl.ds(i * chunk, chunk)]
-        q_ref[pl.ds(i * chunk, chunk)] = dot_nt(
-            jnp.concatenate([block, block[:, :256]], axis=1), scaled
-        ).astype(BF16)
+    scaled_ref[...] = jnp.concatenate([high, high, middle], axis=1)
+    for i in range(EARLY):
+        q_ref[pl.ds(i * chunk, chunk)] = basis(s[pl.ds(i * chunk, chunk)], scaled_ref[...])
     r_ref[...] = jnp.where(above >= 0, m[:, :256] / root, 0.0)
 
     owner = z // 4
@@ -269,18 +271,23 @@
         ahead = [column(r[s + 1][at], lane + 8 + k) for k in range(8)] if s < 7 else []
         scale = jnp.zeros((8, 128), F32)
         for j in range(8):
-            pivot = row(c[s, j], j)
+            pivot = row(c[s, j], j) if j == 0 else following
             inverse = 1.0 / pivot
             scale = jnp.where(sublane == j, lax.rsqrt(pivot), scale)
+            own = c[s, j]
             across = [row(c[s + 1, j], k) for k in range(len(ahead))]
             for g in range(s, 8):
                 c[g, j] = c[g, j] * inverse
             for k in range(len(ahead)):
                 ahead[k] = ahead[k] - c[s + 1, j] * across[k]
             below = jnp.where(sublane > j, c[s, j], 0.0)
+            if j < 7:
+                across = row(c[s, j + 1], j)
+                following = row(c[s, j + 1], j + 1) - across * across * inverse
             for k in range(j + 1, 8):
                 across = row(c[s, k], j)
-                for g in range(s, 8):
+                c[s, k] = c[s, k] - own * across * inverse
+                for g in range(s + 1, 8):
                     c[g, k] = c[g, k] - c[g, j] * across
             for t in range(3):
                 across = row(r[s][t], j)
@@ -308,20 +315,32 @@
         m[low:, width] -= update[low % 128 :]
 
 
-def deliver(q, r, p, q_hbm, r_hbm, p_hbm, sem):
-    copies = [
-        pltpu.make_async_copy(src, dst, sem.at[i])
-        for i, (src, dst) in enumerate([(q, q_hbm), (r, r_hbm), (p, p_hbm)])
-    ]
-    for copy in copies:
-        copy.start()
-    for copy in copies:
-        copy.wait()
+def deliver(q, s, scaled, r, p, q_hbm, r_hbm, p_hbm, late, sem):
+    chunk = s.shape[0] // CHUNKS
+
+    def save(i):
+        src = q.at[pl.ds(i * chunk, chunk)] if i < EARLY else late.at[i - EARLY]
+        return pltpu.make_async_copy(src, q_hbm.at[pl.ds(i * chunk, chunk)], sem.at[i])
+
+    pass_r = pltpu.make_async_copy(r, r_hbm, sem.at[CHUNKS])
+    pass_p = pltpu.make_async_copy(p, p_hbm, sem.at[CHUNKS + 1])
+    for i in range(EARLY):
+        save(i).start()
+    pass_r.start()
+    pass_p.start()
+    for i in range(EARLY, CHUNKS):
+        late[i - EARLY] = basis(s[pl.ds(i * chunk, chunk)], scaled[...])
+        save(i).start()
+    for i in range(CHUNKS):
+        save(i).wait()
+    pass_r.wait()
+    pass_p.wait()
 
 
 def local(archive, sketch):
     pixels, depth = archive.shape
     rank = sketch.shape[1]
+    chunk = pixels // CHUNKS
     root = float(pixels * lax.axis_size("gx") * lax.axis_size("gy")) ** 0.5
     any_spec = pl.BlockSpec(memory_space=pl.ANY)
     vmem = pl.BlockSpec(memory_space=pltpu.VMEM)
@@ -329,16 +348,17 @@
     results = pl.pallas_call(
         functools.partial(exchange, root),
         out_shape=(
-            pltpu.VMEM((pixels, rank), BF16),
+            pltpu.VMEM((EARLY * chunk, rank), BF16),
+            pltpu.VMEM((pixels, 2 * rank), BF16),
+            pltpu.VMEM((rank, 3 * rank), BF16),
             pltpu.VMEM((rank, rank), F32),
             pltpu.VMEM((4, rank), F32),
         ),
         in_specs=[any_spec, any_spec],
-        out_specs=(vmem, vmem, vmem),
+        out_specs=(vmem,) * 5,
         scratch_shapes=[
             pltpu.VMEM((pixels, depth), BF16),
             pltpu.VMEM((depth, rank), BF16),
-            pltpu.VMEM((pixels, 2 * rank), BF16),
             pltpu.VMEM((2 * rank, pixels), BF16),
             pltpu.VMEM((32, 8, 256), F32),
             pltpu.VMEM((16, 8, 256), F32),
@@ -362,11 +382,15 @@
     )(archive, sketch)
     return pl.pallas_call(
         deliver,
-        out_shape=tuple(jax.ShapeDtypeStruct(r.shape, r.dtype) for r in results),
-        in_specs=[vmem] * 3,
+        out_shape=(
+            jax.ShapeDtypeStruct((pixels, rank), BF16),
+            jax.ShapeDtypeStruct((rank, rank), F32),
+            jax.ShapeDtypeStruct((4, rank), F32),
+        ),
+        in_specs=[vmem] * 5,
         out_specs=(any_spec,) * 3,
-        scratch_shapes=[dma((3,))],
-        compiler_params=pltpu.CompilerParams(vmem_limit_bytes=4 * 2**20),
+        scratch_shapes=[pltpu.VMEM((CHUNKS - EARLY, chunk, rank), BF16), dma((CHUNKS + 2,))],
+        compiler_params=pltpu.CompilerParams(vmem_limit_bytes=8 * 2**20),
     )(*results)
 
 

time: 48.3 us -> 46.8 us (0.969)
  Pallas kernels: 47.4 us -> 46 us
    pallas_call x1, Pallas kernels: 46 us -> 43.5 us  [local(): pl.pallas_call(functools.partial(exchange, root), out_shape=(pltpu.VMEM((...]
    pallas_call x1, Pallas kernels: 1.42 us -> 2.44 us  [local(): pl.pallas_call(deliver, out_shape=(jax.ShapeDtypeStruct((pixels, rank), B...]
where the time goes in v7:
time: 46.8 us
  Pallas kernels  46 us (98%)
  between operations  0.8 us (2%)
    pallas_call x1, Pallas kernels, local(): pl.pallas_call(functools.partial(exchange, root), out_shape=(pltpu.VMEM((...  43.5 us
    pallas_call x1, Pallas kernels, local(): pl.pallas_call(deliver, out_shape=(jax.ShapeDtypeStruct((pixels, rank), B...  2.44 us

profile of v7, /device:TPU:1, one launch (start us, length us, event | category | flops | bytes accessed | tf_op | source)
XLA Modules:
  0.0 46.8 jit_solution(15501547863328528490)
XLA Ops:
  0.6 43.5 %shard_map.49 = (bf16[1024,256]{1,0:T(8,128)(2,1)S(1)}, bf16[4096,512]{1,0:T(8,128)(2,1)S(1)}, bf16[256,768]{1,0:T(8,128)(2,1)S(1)}, f32[256,256]{1,0:T(8,128)S(1)}, f32[4,256]{1,0:T(4,128)S(1)}) custom-call(bf16[4096,1024]{1,0:T(8,128)(2,1)} %archive_hbm.1, bf16[1024,256]{1,0:T(8,128)(2,1)} %sketch_hbm.1), custom_call_target="tpu_custom_call" | custom-call | tf_op jit(solution)/shard_map/pallas_call | solution.py:348
  44.2 2.4 %shard_map.50 = (bf16[4096,256]{1,0:T(8,128)(2,1)}, f32[256,256]{1,0:T(8,128)}, f32[4,256]{1,0:T(4,128)}) custom-call(bf16[1024,256]{1,0:T(8,128)(2,1)S(1)} %get-tuple-element.8.q, bf16[4096,512]{1,0:T(8,128)(2,1)S(1)} %get-tuple-element.9.s, bf16[256,768]{1,0:T(8,128)(2,1)S(1)} %get-tuple-element.10.scaled, f32[256,256]{1,0:T(8,128)S(1)} %get-tuple-element.11.r, ...), custom_call_target="tpu_custom_call" | custom-call | tf_op jit(solution)/shard_map/pallas_call | solution.py:383
